TPU v7x, 128 devices: a whole 4x4x4 slice. The times are simulated.
128 devices in a mesh: surf: 4 (over x), norm: 32 (over z, y, core).
Axes of the slice: x: 4, y: 4, z: 4, core: 2. Of those that a mesh axis runs over, the one named last changes fastest.
Arguments:
- rhs: float32 [128, 48, 512], P('norm', None, 'surf'), may hold values from -6 to 6
- previous: float32 [128, 48, 512], P('norm', None, 'surf'), may hold values from -6 to 6
- minus_jac: bfloat16 [128, 48, 48, 512], P('norm', None, None, 'surf'), may hold values from -0.4375 to 0.4375
- plus_jac: bfloat16 [128, 48, 48, 512], P('norm', None, None, 'surf'), may hold values from -0.4375 to 0.4375
- dissipation: float32 [128, 48, 512], P('norm', None, 'surf'), may hold values from 0.01 to 0.08
- inverse_diag: bfloat16 [128, 48, 48, 512], P('norm', None, None, 'surf'), may hold values from -0.078125 to 0.078125
- lower_coupling: bfloat16 [128, 48, 48, 512], P('norm', None, None, 'surf'), may hold values from -0.1484375 to 1, as said below
- upper_coupling: bfloat16 [128, 48, 48, 512], P('norm', None, None, 'surf'), may hold values from -0.1484375 to 1, as said below
Outputs:
- update: float32 [128, 48, 512], P('norm', None, 'surf')
Inputs may be any that keep to these rules, and one draw needn't show every extreme that they name: `lower_coupling`: diagonal entries in (0, 1], off-diagonal entries small. `upper_coupling`: diagonal entries in (0, 1], off-diagonal entries small.
All inputs are finite; a program needn't handle non-finite values.
Results may differ from a plain program's by a relative error of at most 0.0003.
Values may be sent and summed in bfloat16 or wider, within the bound.
No kernel may reach another device: no remote copies, remote signals or barrier semaphores. Data moves between devices by JAX's collectives and lax.ppermute only.
A program may use at most 512 MiB of HBM per device.

v0:
```python
import jax
import jax.numpy as jnp
from jax import lax
from jax.sharding import PartitionSpec as P

SWEEPS = 2


HIGH = lax.Precision.HIGHEST


def with_halo(cells, sides, width):
    for axis, dim in sides:
        count = lax.axis_size(axis)
        ends = count - 1
        head = lax.slice_in_dim(cells, 0, width, axis=dim)
        tail = lax.slice_in_dim(cells, cells.shape[dim] - width, cells.shape[dim], axis=dim)
        cells = jnp.concatenate(
            [
                lax.ppermute(tail, axis, [(i, (i + 1) % count) for i in range(ends)]),
                cells,
                lax.ppermute(head, axis, [((i + 1) % count, i) for i in range(ends)]),
            ],
            axis=dim,
        )
    return cells


def passed_along(value, axis, by):
    length = lax.axis_size(axis)
    pairs = [(i, i + by) for i in range(length) if 0 <= i + by < length]
    return lax.ppermute(value, axis, pairs)


def matvec(block, vector):
    return jnp.einsum("abs,bs->as", block.astype(jnp.float32), vector, precision=HIGH)


def advance(carry, items):
    source_cell, block = items
    value = source_cell + matvec(block, carry)
    return (value, value)


def run_forward(source, cell_block_set, start):
    return lax.scan(advance, start, (source, cell_block_set))[1]


def run_backward(values, cell_block_set, start):
    return lax.scan(advance, start, (values, cell_block_set), reverse=True)[1]


def shards(
    rhs, previous, minus_jac, plus_jac, dissipation, inverse_diag, lower_coupling, upper_coupling
):
    equations = rhs.shape[1]
    width = rhs.shape[2]
    zeros_line = jnp.zeros((equations, width), jnp.float32)
    delta = previous
    for sweep_index in range(SWEEPS):
        padded = with_halo(delta, (("surf", 2),), 2)
        left_two = padded[:, :, 0:width]
        left_one = padded[:, :, 1 : width + 1]
        centre = padded[:, :, 2 : width + 2]
        right_one = padded[:, :, 3 : width + 3]
        right_two = padded[:, :, 4 : width + 4]
        fourth = left_two - 4.0 * left_one + 6.0 * centre - 4.0 * right_one + right_two

        def per_cell(items):
            residual_cell, below, above, minus_block, plus_block, inverse_block = items
            return matvec(
                inverse_block,
                residual_cell - matvec(minus_block, below) - matvec(plus_block, above),
            )

        source = lax.map(
            per_cell,
            (rhs - dissipation * fourth, left_one, right_one, minus_jac, plus_jac, inverse_diag),
        )
        incoming = zeros_line
        for relay_round in range(lax.axis_size("norm") - 1):
            partial_run = run_forward(source, lower_coupling, incoming)
            incoming = passed_along(partial_run[-1], "norm", 1)
        forward_values = run_forward(source, lower_coupling, incoming)
        incoming = zeros_line
        for relay_round in range(lax.axis_size("norm") - 1):
            partial_run = run_backward(forward_values, upper_coupling, incoming)
            incoming = passed_along(partial_run[0], "norm", -1)
        delta = run_backward(forward_values, upper_coupling, incoming)
    return delta


def solution(mesh):
    return jax.shard_map(
        shards,
        mesh=mesh,
        in_specs=(
            P("norm", None, "surf"),
            P("norm", None, "surf"),
            P("norm", None, None, "surf"),
            P("norm", None, None, "surf"),
            P("norm", None, "surf"),
            P("norm", None, None, "surf"),
            P("norm", None, None, "surf"),
            P("norm", None, None, "surf"),
        ),
        out_specs=P("norm", None, "surf"),
        check_vma=False,
    )
```

profile of v0, /device:TPU:31, one launch (start us, length us, event | category | flops | bytes accessed | tf_op | source)
XLA Modules:
  0.0 1321.8 jit_solution(13137214740422644434)
XLA Ops:
  10.3 12.0 while.1816
  30.2 6.3 collective-permute-start.3
  38.3 6.3 collective-permute-start.4
  46.4 6.3 collective-permute-start.5
  54.6 6.3 collective-permute-start.6
  62.7 6.3 collective-permute-start.7
  70.8 6.3 collective-permute-start.8
  78.9 6.3 collective-permute-start.9
  87.0 6.3 collective-permute-start.10
  95.1 6.3 collective-permute-start.11
  103.2 6.3 collective-permute-start.12
  111.4 6.3 collective-permute-start.13
  119.5 6.3 collective-permute-start.14
  127.6 6.3 collective-permute-start.15
  135.7 6.3 collective-permute-start.16
  143.8 6.3 collective-permute-start.17
  151.9 6.3 collective-permute-start.18
  160.0 6.3 collective-permute-start.19
  168.2 6.3 collective-permute-start.20
  176.3 6.3 collective-permute-start.21
  184.4 6.3 collective-permute-start.22
  192.5 6.3 collective-permute-start.23
  200.6 6.3 collective-permute-start.24
  208.7 6.3 collective-permute-start.25
  216.8 6.3 collective-permute-start.26
  225.0 6.3 collective-permute-start.27
  233.1 6.3 collective-permute-start.28
  241.2 6.3 collective-permute-start.29
  249.3 6.3 collective-permute-start.30
  257.4 6.3 collective-permute-start.31
  265.5 6.3 collective-permute-start.32
  280.7 5.9 collective-permute-done.33
  670.3 12.0 while.1879
  688.3 6.3 collective-permute-start.67
  696.4 6.3 collective-permute-start.68
  704.5 6.3 collective-permute-start.69
  712.7 6.3 collective-permute-start.70
  720.8 6.3 collective-permute-start.71
  728.9 6.3 collective-permute-start.72
  737.0 6.3 collective-permute-start.73
  745.1 6.3 collective-permute-start.74
  753.2 6.3 collective-permute-start.75
  761.3 6.3 collective-permute-start.76
  769.5 6.3 collective-permute-start.77
  777.6 6.5 collective-permute-start.78
  785.9 6.3 collective-permute-start.79
  794.0 6.3 collective-permute-start.80
  802.1 6.3 collective-permute-start.81
  810.2 6.3 collective-permute-start.82
  818.3 6.3 collective-permute-start.83
  826.5 6.3 collective-permute-start.84
  834.6 6.3 collective-permute-start.85
  842.7 6.3 collective-permute-start.86
  850.8 6.3 collective-permute-start.87
  858.9 6.3 collective-permute-start.88
  867.0 6.3 collective-permute-start.89
  875.1 6.3 collective-permute-start.90
  883.3 6.3 collective-permute-start.91
  891.4 6.3 collective-permute-start.92
  899.5 6.3 collective-permute-start.93
  907.6 6.3 collective-permute-start.94
  915.7 6.3 collective-permute-start.95
  923.8 6.3 collective-permute-start.96
  939.0 5.9 collective-permute-done.97
  (1684 shorter events, 1288.2 us)
Async XLA Ops:
  30.2 7.3 collective-permute-start.3
  38.3 7.3 collective-permute-start.4
  46.4 7.3 collective-permute-start.5
  54.6 7.3 collective-permute-start.6
  62.7 7.3 collective-permute-start.7
  70.8 7.3 collective-permute-start.8
  78.9 7.3 collective-permute-start.9
  87.0 7.3 collective-permute-start.10
  95.1 7.3 collective-permute-start.11
  103.2 7.3 collective-permute-start.12
  111.4 7.3 collective-permute-start.13
  119.5 7.3 collective-permute-start.14
  127.6 7.3 collective-permute-start.15
  135.7 7.3 collective-permute-start.16
  143.8 7.3 collective-permute-start.17
  151.9 7.3 collective-permute-start.18
  160.0 7.3 collective-permute-start.19
  168.2 7.3 collective-permute-start.20
  176.3 7.3 collective-permute-start.21
  184.4 7.3 collective-permute-start.22
  192.5 7.3 collective-permute-start.23
  200.6 7.3 collective-permute-start.24
  208.7 7.3 collective-permute-start.25
  216.8 7.3 collective-permute-start.26
  225.0 7.3 collective-permute-start.27
  233.1 7.3 collective-permute-start.28
  241.2 7.3 collective-permute-start.29
  249.3 7.3 collective-permute-start.30
  257.4 7.3 collective-permute-start.31
  265.5 7.3 collective-permute-start.32
  278.8 7.8 collective-permute-start.33
  440.0 7.3 collective-permute-start.46
  464.7 7.3 collective-permute-start.48
  688.3 7.3 collective-permute-start.67
  696.4 7.3 collective-permute-start.68
  704.5 7.3 collective-permute-start.69
  712.7 7.3 collective-permute-start.70
  720.8 7.3 collective-permute-start.71
  728.9 7.3 collective-permute-start.72
  737.0 7.3 collective-permute-start.73
  745.1 7.3 collective-permute-start.74
  753.2 7.3 collective-permute-start.75
  761.3 7.3 collective-permute-start.76
  769.5 7.3 collective-permute-start.77
  777.6 7.5 collective-permute-start.78
  785.9 7.3 collective-permute-start.79
  794.0 7.3 collective-permute-start.80
  802.1 7.3 collective-permute-start.81
  810.2 7.3 collective-permute-start.82
  818.3 7.3 collective-permute-start.83
  826.5 7.3 collective-permute-start.84
  834.6 7.3 collective-permute-start.85
  842.7 7.3 collective-permute-start.86
  850.8 7.3 collective-permute-start.87
  858.9 7.3 collective-permute-start.88
  867.0 7.3 collective-permute-start.89
  875.1 7.3 collective-permute-start.90
  883.3 7.3 collective-permute-start.91
  891.4 7.3 collective-permute-start.92
  899.5 7.3 collective-permute-start.93
  907.6 7.3 collective-permute-start.94
  915.7 7.3 collective-permute-start.95
  923.8 7.3 collective-permute-start.96
  937.1 7.8 collective-permute-start.97
  (68 other events, 490.1 us)
where the time goes:
time: 1350 us; the launch traced here: 1320 us
  starting transfers between devices  516 us (38%)
  waiting for transfers between devices  396 us (29%)
  other arithmetic  388 us (29%)
  loops' own time  13.8 us (1%)
    ppermute x124, starting transfers between devices, passed_along(): return lax.ppermute(value, axis, pairs)  509 us
    ppermute x124, waiting for transfers between devices, passed_along(): return lax.ppermute(value, axis, pairs)  388 us
    dot_general x528, other arithmetic, matvec(): jnp.einsum('abs,bs->as', block.astype(jnp.float32), vector, precision=HIGH)  378 us
  transfers between devices with their start and end apart: 128, of which 127 were waited for; matrix products, arithmetic and copies ran while one was open for 0% of the time, Pallas kernels for 0%

commit v1 on v0

v1 whole, which is shorter than its diff:
```python
import functools

import jax
import jax.numpy as jnp
from jax import lax
from jax.experimental import pallas as pl
from jax.experimental.pallas import tpu as pltpu
from jax.sharding import PartitionSpec as P

SWEEPS = 2
N = 48
CELLS = 4
LANES = 128
MAT = N * N
GROUPS = 32
COLS = LANES // GROUPS
ROWS = 72
VEC = 3 * ROWS
PACK = VEC + 8
F32 = jnp.float32
BF16 = jnp.bfloat16
LIMIT = 60 * 1024 * 1024


def params():
    return pltpu.CompilerParams(vmem_limit_bytes=LIMIT)


def whole():
    return pl.BlockSpec(memory_space=pltpu.VMEM)


def matmul_cells(left, right, out, add=None):
    def block(step, carry):
        base = pl.multiple_of(step * 4 * N, 8)
        sums = [None] * 4
        for b in range(N):
            vector = right[pl.ds(b * N, N), :]
            for k in range(4):
                term = left[pl.ds(base + k * N + b, 1), :] * vector
                sums[k] = term if sums[k] is None else sums[k] + term
        for k in range(4):
            where = pl.ds(pl.multiple_of(base + k * N, 8), N)
            value = sums[k]
            if add is not None:
                value = value + add[where, :]
            out[where, :] = value
        return carry

    lax.fori_loop(0, N // 4, block, 0)


def pack_matrix(mat, out, first):
    def column(c, lo, count):
        return mat[pl.ds(c + lo * N, count, stride=N), :]

    def main(r, carry):
        tile = jnp.concatenate(
            [column(r, 0, 48), column(32 + r, 0, 16), column(16 + r, 0, 48), column(32 + r, 16, 16)], axis=0
        ).T
        for i in range(COLS):
            out[pl.ds(first + i * 16 + r, GROUPS, stride=PACK), :] = tile[GROUPS * i : GROUPS * (i + 1)]
        return carry

    lax.fori_loop(0, 16, main, 0)

    def rest(r, carry):
        tile = jnp.concatenate(
            [column(32 + r, 32, 16), column(40 + r, 32, 16), jnp.zeros((96, LANES), F32)], axis=0
        ).T
        out[pl.ds(first + 64 + r, GROUPS, stride=PACK), :] = jnp.concatenate(
            [tile[GROUPS * i : GROUPS * (i + 1), 0:32] for i in range(COLS)], axis=1
        )
        return carry

    lax.fori_loop(0, 8, rest, 0)


def products_kernel(lower, upper, out, low, upp, work0, work1, work2, work3):
    for k in range(CELLS):
        def widen(r, carry):
            where = pl.ds(pl.multiple_of(r * N, 16), N)
            low[k, where, :] = lower[k, r].astype(F32)
            upp[k, where, :] = upper[k, r].astype(F32)
            return carry

        lax.fori_loop(0, N, widen, 0)
    matmul_cells(low.at[1], low.at[0], work0)
    matmul_cells(low.at[2], work0, work1)
    matmul_cells(low.at[3], work1, work2)
    pack_matrix(work2, out, 0)
    matmul_cells(upp.at[2], work2, work3, work1)
    matmul_cells(upp.at[1], work3, work1, work0)
    matmul_cells(upp.at[0], work1, work2, low.at[0])
    pack_matrix(work2, out, 2 * ROWS)
    matmul_cells(upp.at[2], upp.at[3], work0)
    matmul_cells(upp.at[1], work0, work1)
    matmul_cells(upp.at[0], work1, work2)
    pack_matrix(work2, out, ROWS)


def products(lower, upper):
    return pl.pallas_call(
        products_kernel,
        out_shape=jax.ShapeDtypeStruct((GROUPS * PACK, LANES), F32),
        in_specs=[whole(), whole()],
        out_specs=whole(),
        scratch_shapes=[pltpu.VMEM((CELLS, MAT, LANES), F32)] * 2 + [pltpu.VMEM((MAT, LANES), F32)] * 4,
        compiler_params=params(),
        name="products",
    )(lower, upper)


def matvec(block, vector):
    rows = []
    for a in range(N):
        part = block[a].astype(F32) * vector
        rows.append(jnp.sum(part, axis=0, keepdims=True))
    return jnp.concatenate(rows, axis=0)


def source_kernel(
    rhs, delta, below, above, minus, plus, dissipation, inverse, lower, upper, source, vectors, hold
):
    lane = lax.broadcasted_iota(jnp.int32, (N, LANES), 1)
    forward = jnp.zeros((N, LANES), F32)
    for k in range(CELLS):
        centre = delta[k]
        left = below[k]
        right = above[k]

        def shifted(by):
            here = pltpu.roll(centre, by % LANES, 1)
            if by > 0:
                return jnp.where(lane < by, pltpu.roll(left, by, 1), here)
            return jnp.where(lane >= LANES + by, pltpu.roll(right, by % LANES, 1), here)

        left_one, right_one = shifted(1), shifted(-1)
        fourth = shifted(2) - 4.0 * left_one + 6.0 * centre - 4.0 * right_one + shifted(-2)
        residual = rhs[k] - dissipation[k] * fourth
        residual = residual - matvec(minus.at[k], left_one) - matvec(plus.at[k], right_one)
        value = matvec(inverse.at[k], residual)
        source[k] = value
        forward = value + matvec(lower.at[k], forward) if k else value
        hold[k] = forward
    backward = hold[CELLS - 1]
    for k in range(CELLS - 2, -1, -1):
        backward = hold[k] + matvec(upper.at[k], backward)
    gap = jnp.zeros((16, LANES), F32)
    for row, value in ((0, forward), (COLS, backward)):
        tile = jnp.concatenate([value, gap, value, gap], axis=0).T
        for i in range(COLS):
            vectors[pl.ds(row + i, GROUPS, stride=8), :] = tile[GROUPS * i : GROUPS * (i + 1)]


def local_source(*arrays):
    return pl.pallas_call(
        source_kernel,
        out_shape=(
            jax.ShapeDtypeStruct((CELLS, N, LANES), F32),
            jax.ShapeDtypeStruct((GROUPS * 8, LANES), F32),
        ),
        in_specs=[whole()] * 10,
        out_specs=(whole(), whole()),
        scratch_shapes=[pltpu.VMEM((CELLS, N, LANES), F32)],
        compiler_params=params(),
        name="local_source",
    )(*arrays)


def finish_kernel(incoming, source, lower, upper, delta, hold):
    def incoming_line(row):
        rows = [incoming[pl.ds(row + i, GROUPS, stride=8), :] for i in range(COLS)]
        return jnp.concatenate(rows, axis=0).T[0:N]

    value = incoming_line(0)
    for k in range(CELLS):
        value = source[k] + matvec(lower.at[k], value)
        hold[k] = value
    value = incoming_line(COLS)
    for k in range(CELLS - 1, -1, -1):
        value = hold[k] + matvec(upper.at[k], value)
        delta[k] = value


def finish(*arrays):
    return pl.pallas_call(
        finish_kernel,
        out_shape=jax.ShapeDtypeStruct((CELLS, N, LANES), F32),
        in_specs=[whole()] * 4,
        out_specs=whole(),
        scratch_shapes=[pltpu.VMEM((CELLS, N, LANES), F32)],
        compiler_params=params(),
        name="finish",
    )(*arrays)


def split(value):
    high = value.astype(BF16)
    return high, (value - high.astype(F32)).astype(BF16)


def unpack_matrix(packed, d, first, weights):
    lane = lax.broadcasted_iota(jnp.int32, (16, LANES), 1)
    extra = packed[d, pl.ds(first + 64, 8), :]
    zeros = jnp.zeros((16, LANES), F32)
    for i in range(COLS):
        block = packed[d, pl.ds(first + 16 * i, 16), :]
        turned = pltpu.roll(block, 64, 1)
        low = jnp.where(lane < 64, block, turned)
        high = jnp.where(lane < 64, turned, block)
        tail = jnp.concatenate(
            [pltpu.roll(extra, (32 - 32 * i) % LANES, 1), pltpu.roll(extra, (16 - 32 * i) % LANES, 1)], axis=0
        )
        third = jnp.where(lane < 16, pltpu.roll(block, 80, 1), jnp.where(lane < 32, pltpu.roll(block, 32, 1), tail))
        third = jnp.where(lane < 64, third, pltpu.roll(third, 64, 1))
        both = jnp.concatenate([low, high, third, zeros], axis=0)
        first_part, second_part = split(both)
        weights[pl.ds(64 * i, 64), 0:LANES] = first_part
        weights[pl.ds(64 * i, 64), LANES : 2 * LANES] = second_part


def spread(value):
    row = lax.broadcasted_iota(jnp.int32, (8, 2 * LANES), 0)
    place = lax.broadcasted_iota(jnp.int32, (8, 2 * LANES), 1) // 64
    keep = jnp.logical_and(row == place, lax.rem(lax.broadcasted_iota(jnp.int32, (8, 2 * LANES), 1), 64) < N)
    wide = jnp.where(keep, jnp.concatenate([value, value], axis=1), 0.0)
    high = wide.astype(BF16).astype(F32)
    return jnp.concatenate([high, wide - high], axis=0).astype(BF16)


def apply(left, weights):
    out = jnp.dot(left, weights[...], preferred_element_type=F32)
    return (out[0:8, 0:LANES] + out[8:16, 0:LANES]) + (out[0:8, LANES:] + out[8:16, LANES:])


def solve_kernel(packed, vectors, out, weights_a, weights_g, weights_b, ends):
    row = lax.broadcasted_iota(jnp.int32, (8, LANES), 0)
    state = jnp.zeros((8, LANES), F32)

    def forward(d, state):
        unpack_matrix(packed, d, 0, weights_a)
        unpack_matrix(packed, d, 2 * ROWS, weights_g)
        left = spread(state)
        ends[d] = pltpu.roll(vectors[d], COLS, 0) + apply(left, weights_g)
        out[d] = state
        return vectors[d] + apply(left, weights_a)

    lax.fori_loop(0, GROUPS, forward, state)

    def backward(e, state):
        d = GROUPS - 1 - e
        unpack_matrix(packed, d, ROWS, weights_b)
        out[d] = jnp.where(row < COLS, out[d], pltpu.roll(state, COLS, 0))
        return ends[d] + apply(spread(state), weights_b)

    lax.fori_loop(0, GROUPS, backward, jnp.zeros((8, LANES), F32))


def solve(packed, vectors):
    return pl.pallas_call(
        solve_kernel,
        out_shape=jax.ShapeDtypeStruct((GROUPS, 8, LANES), F32),
        in_specs=[whole(), whole()],
        out_specs=whole(),
        scratch_shapes=[pltpu.VMEM((2 * LANES, 2 * LANES), BF16)] * 3 + [pltpu.VMEM((GROUPS, 8, LANES), F32)],
        compiler_params=params(),
        name="solve",
    )(packed, vectors)


def exchange(value):
    return lax.all_to_all(value, "norm", 0, 0, tiled=True)


def shards(
    rhs, previous, minus_jac, plus_jac, dissipation, inverse_diag, lower_coupling, upper_coupling
):
    ends = lax.axis_size("surf") - 1
    up = [(i, i + 1) for i in range(ends)]
    down = [(i + 1, i) for i in range(ends)]
    packed = exchange(products(lower_coupling, upper_coupling).reshape(GROUPS, PACK, LANES))
    delta = previous
    for sweep_index in range(SWEEPS):
        below = lax.ppermute(delta, "surf", up)
        above = lax.ppermute(delta, "surf", down)
        source, vectors = local_source(
            rhs, delta, below, above, minus_jac, plus_jac, dissipation, inverse_diag, lower_coupling, upper_coupling
        )
        vectors = exchange(vectors.reshape(GROUPS, 8, LANES))
        incoming = exchange(solve(packed, vectors))
        delta = finish(incoming.reshape(GROUPS * 8, LANES), source, lower_coupling, upper_coupling)
    return delta


def solution(mesh):
    line = P("norm", None, "surf")
    block = P("norm", None, None, "surf")
    return jax.shard_map(
        shards,
        mesh=mesh,
        in_specs=(line, line, block, block, line, block, block, block),
        out_specs=line,
        check_vma=False,
    )
```

time: 1350 us -> 247 us (0.18)
  the two profiles are of different devices: /device:TPU:31 before, /device:TPU:1 now
where the time goes in v1:
time: 247 us; the launch traced here: 246 us
  Pallas kernels  125 us (51%)
  blocking collectives  91.2 us (37%)
  starting transfers between devices  20 us (8%)
  waiting for transfers between devices  8.36 us (3%)
    all_to_all x4, blocking collectives, exchange(): return lax.all_to_all(value, 'norm', 0, 0, tiled=True)  91.2 us
    pallas_call x1, Pallas kernels, products(): pl.pallas_call(products_kernel, out_shape=jax.ShapeDtypeStruct((GROUPS *...  54.1 us
    pallas_call x2, Pallas kernels, solve(): pl.pallas_call(solve_kernel, out_shape=jax.ShapeDtypeStruct((GROUPS, 8, L...  45.9 us
    pallas_call x2, Pallas kernels, local_source(): pl.pallas_call(source_kernel, out_shape=(jax.ShapeDtypeStruct((CELLS, N,...  16.4 us
    all_to_all x1, starting transfers between devices, exchange(): return lax.all_to_all(value, 'norm', 0, 0, tiled=True)  10.2 us
    pallas_call x2, Pallas kernels, finish(): pl.pallas_call(finish_kernel, out_shape=jax.ShapeDtypeStruct((CELLS, N, L...  8.88 us
    ppermute x2, waiting for transfers between devices, shards(): above = lax.ppermute(delta, 'surf', down)  7.14 us
    ppermute x2, starting transfers between devices, shards(): below = lax.ppermute(delta, 'surf', up)  7.04 us
  transfers between devices with their start and end apart: 5, of which 4 were waited for; matrix products, arithmetic and copies ran while one was open for 0% of the time, Pallas kernels for 22%

profile of v1, /device:TPU:1, one launch (start us, length us, event | category | flops | bytes accessed | tf_op | source)
XLA Modules:
  0.0 246.2 jit_solution(1890857927529565897)
XLA Ops:
  0.0 3.9 %collective-permute-start = (f32[4,48,128]{2,1,0:T(8,128)}, f32[4,48,128]{2,1,0:T(8,128)S(1)}, u32[]{:S(2)}, u32[]{:S(2)}) collective-permute-start(f32[4,48,128]{2,1,0:T(8,128)} %delta.1), channel_id=1, source_target_pairs={{0,32},{32,64},{64,96},{1,33},{33,65},{65,97},{2,34},{34,66},{66,9... | collective-permute-start | bytes 294920 | tf_op jit(solution)/shard_map/ppermute | solution.py:285
  3.9 1.3 collective-permute-start.1
  5.2 0.6 collective-permute-done.below
  5.9 0.0 copy-start.2
  5.9 3.6 %collective-permute-done.1.above = f32[4,48,128]{2,1,0:T(8,128)S(1)} collective-permute-done((f32[4,48,128]{2,1,0:T(8,128)}, f32[4,48,128]{2,1,0:T(8,128)S(1)}, u32[]{:S(2)}, u32[]{:S(2)}) %collective-permute-start.1) | collective-permute-done | bytes 98336 | tf_op jit(solution)/shard_map/ppermute | solution.py:286
  9.5 0.0 copy-done.2
  9.5 0.0 copy-start.4
  9.5 0.6 copy-done.4
  10.2 8.2 %local_source.2 = (f32[4,48,128]{2,1,0:T(8,128)}, f32[256,128]{1,0:T(8,128)}) custom-call(f32[4,48,128]{2,1,0:T(8,128)} %rhs.3, f32[4,48,128]{2,1,0:T(8,128)} %delta.1, f32[4,48,128]{2,1,0:T(8,128)} %copy-done.2, f32[4,48,128]{2,1,0:T(8,128)} %copy-done.4, bf16[4,48,48,128]{3,2,1,0:T(8,128)(2,1)} %minus.3, bf16[4,48,48,128]{3,2,1,0:T(8,128)(2,1)} %plus.3, ...), custom_call_target="tpu_custom_call" | custom-call | tf_op jit(solution)/shard_map/local_source/pallas_call | solution.py:157
  18.4 10.2 %all-to-all-start.1 = ((f32[32,8,128]{2,1,0:T(8,128)}), f32[32,8,128]{2,1,0:T(8,128)S(1)}, u32[]{:S(2)}, u32[]{:S(2)}) async-start(f32[32,8,128]{2,1,0:T(8,128)} %bitcast.8), calls=%async_computation.1 | async-start | bytes 262144 | tf_op jit(solution)/shard_map/all_to_all | solution.py:273
  28.6 54.1 %products.1 = f32[7168,128]{1,0:T(8,128)} custom-call(bf16[4,48,48,128]{3,2,1,0:T(8,128)(2,1)} %lower.9, bf16[4,48,48,128]{3,2,1,0:T(8,128)(2,1)} %upper.9), custom_call_target="tpu_custom_call" | custom-call | tf_op jit(solution)/shard_map/products/pallas_call | solution.py:103
  82.7 0.0 all-to-all-done.1.vectors
  82.7 0.0 copy-start
  82.7 52.7 %all_to_all.25.packed = f32[32,224,128]{2,1,0:T(8,128)} all-to-all(f32[32,224,128]{2,1,0:T(8,128)} %bitcast.5), channel_id=1, replica_groups=mesh['surf'=4,'norm'=32] {'norm'}, dimensions={0} | all-to-all | bytes 7340032 | tf_op jit(solution)/shard_map/all_to_all | solution.py:273
  135.5 0.0 copy-done
  135.5 22.9 %solve.2 = f32[32,8,128]{2,1,0:T(8,128)} custom-call(f32[32,224,128]{2,1,0:T(8,128)} %all_to_all.25.packed, f32[32,8,128]{2,1,0:T(8,128)} %copy-done), custom_call_target="tpu_custom_call" | custom-call | tf_op jit(solution)/shard_map/solve/pallas_call | solution.py:261
  158.4 12.4 %all_to_all.26 = f32[32,8,128]{2,1,0:T(8,128)} all-to-all(f32[32,8,128]{2,1,0:T(8,128)} %solve.2), channel_id=1, replica_groups=mesh['surf'=4,'norm'=32] {'norm'}, dimensions={0} | all-to-all | bytes 262144 | tf_op jit(solution)/shard_map/all_to_all | solution.py:273
  170.8 4.4 %finish.2.delta = f32[4,48,128]{2,1,0:T(8,128)} custom-call(f32[256,128]{1,0:T(8,128)} %bitcast.6, f32[4,48,128]{2,1,0:T(8,128)} %get-tuple-element.10.source, bf16[4,48,48,128]{3,2,1,0:T(8,128)(2,1)} %lower.9, bf16[4,48,48,128]{3,2,1,0:T(8,128)(2,1)} %upper.9), custom_call_target="tpu_custom_call" | custom-call | tf_op jit(solution)/shard_map/finish/pallas_call | solution.py:187
  175.2 3.1 %collective-permute-start.2 = (f32[4,48,128]{2,1,0:T(8,128)}, f32[4,48,128]{2,1,0:T(8,128)S(1)}, u32[]{:S(2)}, u32[]{:S(2)}) collective-permute-start(f32[4,48,128]{2,1,0:T(8,128)} %finish.2.delta), channel_id=1, source_target_pairs={{0,32},{32,64},{64,96},{1,33},{33,65},{65,97},{2,34},{34,66},{66,9... | collective-permute-start | bytes 294920 | tf_op jit(solution)/shard_map/ppermute | solution.py:285
  178.3 1.5 collective-permute-start.3
  179.8 0.6 collective-permute-done.2.below
  180.4 0.0 copy-start.1
  180.4 3.5 %collective-permute-done.3.above = f32[4,48,128]{2,1,0:T(8,128)S(1)} collective-permute-done((f32[4,48,128]{2,1,0:T(8,128)}, f32[4,48,128]{2,1,0:T(8,128)S(1)}, u32[]{:S(2)}, u32[]{:S(2)}) %collective-permute-start.3) | collective-permute-done | bytes 98336 | tf_op jit(solution)/shard_map/ppermute | solution.py:286
  183.9 0.0 copy-done.1
  183.9 0.0 copy-start.3
  183.9 0.6 copy-done.3
  184.5 8.2 %local_source.3 = (f32[4,48,128]{2,1,0:T(8,128)}, f32[256,128]{1,0:T(8,128)}) custom-call(f32[4,48,128]{2,1,0:T(8,128)} %rhs.3, f32[4,48,128]{2,1,0:T(8,128)} %finish.2.delta, f32[4,48,128]{2,1,0:T(8,128)} %copy-done.1, f32[4,48,128]{2,1,0:T(8,128)} %copy-done.3, bf16[4,48,48,128]{3,2,1,0:T(8,128)(2,1)} %minus.3, bf16[4,48,48,128]{3,2,1,0:T(8,128)(2,1)} %plus.3, ...), custom_call_target="tpu_custom_call" | custom-call | tf_op jit(solution)/shard_map/local_source/pallas_call | solution.py:157
  192.8 13.8 %all_to_all.27.vectors = f32[32,8,128]{2,1,0:T(8,128)} all-to-all(f32[32,8,128]{2,1,0:T(8,128)} %bitcast.9), channel_id=1, replica_groups=mesh['surf'=4,'norm'=32] {'norm'}, dimensions={0} | all-to-all | bytes 262144 | tf_op jit(solution)/shard_map/all_to_all | solution.py:273
  206.5 22.9 %solve.3 = f32[32,8,128]{2,1,0:T(8,128)} custom-call(f32[32,224,128]{2,1,0:T(8,128)} %all_to_all.25.packed, f32[32,8,128]{2,1,0:T(8,128)} %all_to_all.27.vectors), custom_call_target="tpu_custom_call" | custom-call | tf_op jit(solution)/shard_map/solve/pallas_call | solution.py:261
  229.5 12.3 %all_to_all.28 = f32[32,8,128]{2,1,0:T(8,128)} all-to-all(f32[32,8,128]{2,1,0:T(8,128)} %solve.3), channel_id=1, replica_groups=mesh['surf'=4,'norm'=32] {'norm'}, dimensions={0} | all-to-all | bytes 262144 | tf_op jit(solution)/shard_map/all_to_all | solution.py:273
  241.8 4.4 %finish.3 = f32[4,48,128]{2,1,0:T(8,128)} custom-call(f32[256,128]{1,0:T(8,128)} %bitcast.7, f32[4,48,128]{2,1,0:T(8,128)} %get-tuple-element.12.source, bf16[4,48,48,128]{3,2,1,0:T(8,128)(2,1)} %lower.9, bf16[4,48,48,128]{3,2,1,0:T(8,128)(2,1)} %upper.9), custom_call_target="tpu_custom_call" | custom-call | tf_op jit(solution)/shard_map/finish/pallas_call | solution.py:187
Async XLA Ops:
  0.0 5.9 %collective-permute-start = (f32[4,48,128]{2,1,0:T(8,128)}, f32[4,48,128]{2,1,0:T(8,128)S(1)}, u32[]{:S(2)}, u32[]{:S(2)}) collective-permute-start(f32[4,48,128]{2,1,0:T(8,128)} %delta.1), channel_id=1, source_target_pairs={{0,32},{32,64},{64,96},{1,33},{33,65},{65,97},{2,34},{34,66},{66,9... | collective-permute-start | bytes 294920 | tf_op jit(solution)/shard_map/ppermute | solution.py:285
  3.9 5.6 %collective-permute-start.1 = (f32[4,48,128]{2,1,0:T(8,128)}, f32[4,48,128]{2,1,0:T(8,128)S(1)}, u32[]{:S(2)}, u32[]{:S(2)}) collective-permute-start(f32[4,48,128]{2,1,0:T(8,128)} %delta.1), channel_id=1, source_target_pairs={{32,0},{64,32},{96,64},{33,1},{65,33},{97,65},{34,2},{66,34},{98,6... | collective-permute-start | bytes 294920 | tf_op jit(solution)/shard_map/ppermute | solution.py:286
  5.9 3.6 %copy-start.2 = (f32[4,48,128]{2,1,0:T(8,128)}, f32[4,48,128]{2,1,0:T(8,128)S(1)}, u32[]{:S(2)}) copy-start(f32[4,48,128]{2,1,0:T(8,128)S(1)} %collective-permute-done.below) | copy-start | bytes 294916
  9.5 0.6 copy-start.4
  18.4 64.3 %all-to-all-start.1 = ((f32[32,8,128]{2,1,0:T(8,128)}), f32[32,8,128]{2,1,0:T(8,128)S(1)}, u32[]{:S(2)}, u32[]{:S(2)}) async-start(f32[32,8,128]{2,1,0:T(8,128)} %bitcast.8), calls=%async_computation.1 | async-start | bytes 262144 | tf_op jit(solution)/shard_map/all_to_all | solution.py:273
  82.7 52.8 %copy-start = (f32[32,8,128]{2,1,0:T(8,128)}, f32[32,8,128]{2,1,0:T(8,128)S(1)}, u32[]{:S(2)}) copy-start(f32[32,8,128]{2,1,0:T(8,128)S(1)} %all-to-all-done.1.vectors) | copy-start | bytes 393220
  175.2 5.2 %collective-permute-start.2 = (f32[4,48,128]{2,1,0:T(8,128)}, f32[4,48,128]{2,1,0:T(8,128)S(1)}, u32[]{:S(2)}, u32[]{:S(2)}) collective-permute-start(f32[4,48,128]{2,1,0:T(8,128)} %finish.2.delta), channel_id=1, source_target_pairs={{0,32},{32,64},{64,96},{1,33},{33,65},{65,97},{2,34},{34,66},{66,9... | collective-permute-start | bytes 294920 | tf_op jit(solution)/shard_map/ppermute | solution.py:285
  178.3 5.6 %collective-permute-start.3 = (f32[4,48,128]{2,1,0:T(8,128)}, f32[4,48,128]{2,1,0:T(8,128)S(1)}, u32[]{:S(2)}, u32[]{:S(2)}) collective-permute-start(f32[4,48,128]{2,1,0:T(8,128)} %finish.2.delta), channel_id=1, source_target_pairs={{32,0},{64,32},{96,64},{33,1},{65,33},{97,65},{34,2},{66,34},{98,6... | collective-permute-start | bytes 294920 | tf_op jit(solution)/shard_map/ppermute | solution.py:286
  180.4 3.5 %copy-start.1 = (f32[4,48,128]{2,1,0:T(8,128)}, f32[4,48,128]{2,1,0:T(8,128)S(1)}, u32[]{:S(2)}) copy-start(f32[4,48,128]{2,1,0:T(8,128)S(1)} %collective-permute-done.2.below) | copy-start | bytes 294916
  183.9 0.6 copy-start.3

commit v2 on v1

v2 whole, which is shorter than its diff:
```python
import functools

import jax
import jax.numpy as jnp
from jax import lax
from jax.experimental import pallas as pl
from jax.experimental.pallas import tpu as pltpu
from jax.sharding import PartitionSpec as P

SWEEPS = 2
N = 48
CELLS = 4
LANES = 128
MAT = N * N
GROUPS = 32
COLS = LANES // GROUPS
ROWS = 72
FIRST = ROWS + 8
F32 = jnp.float32
BF16 = jnp.bfloat16


def params(mebibytes, microseconds):
    cost = pl.CostEstimate(flops=int(microseconds * 1e9), bytes_accessed=0, transcendentals=0)
    return dict(
        compiler_params=pltpu.CompilerParams(vmem_limit_bytes=mebibytes * 1024 * 1024), cost_estimate=cost
    )


def whole():
    return pl.BlockSpec(memory_space=pltpu.VMEM)


def matmul_cells(left, right, out, add=None):
    def block(step, carry):
        base = pl.multiple_of(step * 4 * N, 8)
        sums = [None] * 4
        for b in range(N):
            vector = right[pl.ds(b * N, N), :]
            for k in range(4):
                term = left[pl.ds(base + k * N + b, 1), :] * vector
                sums[k] = term if sums[k] is None else sums[k] + term
        for k in range(4):
            where = pl.ds(pl.multiple_of(base + k * N, 8), N)
            value = sums[k]
            if add is not None:
                value = value + add[where, :]
            out[where, :] = value
        return carry

    lax.fori_loop(0, N // 4, block, 0)


def pack_matrix(mat, out, first, pitch):
    def column(c, lo, count):
        return mat[pl.ds(c + lo * N, count, stride=N), :]

    def main(r, carry):
        tile = jnp.concatenate(
            [column(r, 0, 48), column(32 + r, 0, 16), column(16 + r, 0, 48), column(32 + r, 16, 16)], axis=0
        ).T
        for i in range(COLS):
            out[pl.ds(first + i * 16 + r, GROUPS, stride=pitch), :] = tile[GROUPS * i : GROUPS * (i + 1)]
        return carry

    lax.fori_loop(0, 16, main, 0, unroll=4)

    def rest(r, carry):
        tile = jnp.concatenate(
            [column(32 + r, 32, 16), column(40 + r, 32, 16), jnp.zeros((96, LANES), F32)], axis=0
        ).T
        out[pl.ds(first + 64 + r, GROUPS, stride=pitch), :] = jnp.concatenate(
            [tile[GROUPS * i : GROUPS * (i + 1), 0:32] for i in range(COLS)], axis=1
        )
        return carry

    lax.fori_loop(0, 8, rest, 0, unroll=4)


def widen(narrow, wide):
    for k in range(CELLS):
        def row(r, carry):
            wide[k, pl.ds(pl.multiple_of(r * N, 16), N), :] = narrow[k, r].astype(F32)
            return carry

        lax.fori_loop(0, N, row, 0, unroll=4)


def anywhere():
    return pl.BlockSpec(memory_space=pl.ANY)


def forward_kernel(lower, after, out, chain, low, work, sems):
    widen(lower, low)
    copies = []

    def keep(k, ref):
        copies.append(pltpu.make_async_copy(ref, chain.at[k], sems.at[k]))
        copies[-1].start()

    keep(0, low.at[0])
    for k in range(1, CELLS):
        before = low.at[0] if k == 1 else work.at[k - 2]
        matmul_cells(low.at[k], before, work.at[k - 1])
        keep(k, work.at[k - 1])
    pack_matrix(work.at[CELLS - 2], out, 0, FIRST)
    for copy in copies:
        copy.wait()


def forward_products(lower, after):
    return pl.pallas_call(
        forward_kernel,
        out_shape=(
            jax.ShapeDtypeStruct((GROUPS * FIRST, LANES), F32),
            jax.ShapeDtypeStruct((CELLS, MAT, LANES), F32),
        ),
        in_specs=[whole(), anywhere()],
        out_specs=(whole(), anywhere()),
        scratch_shapes=[
            pltpu.VMEM((CELLS, MAT, LANES), F32),
            pltpu.VMEM((CELLS - 1, MAT, LANES), F32),
            pltpu.SemaphoreType.DMA((CELLS,)),
        ],
        name="forward_products",
        **params(20, 12),
    )(lower, after)


def backward_kernel(upper, after, out, upp, work0, work1):
    widen(upper, upp)
    matmul_cells(upp.at[2], upp.at[3], work0)
    matmul_cells(upp.at[1], work0, work1)
    matmul_cells(upp.at[0], work1, work0)
    pack_matrix(work0, out, 0, ROWS)


def across_kernel(upper, after, chain, out, upp, have, work0, work1, sems):
    copies = [pltpu.make_async_copy(chain.at[k], have.at[k], sems.at[k]) for k in range(CELLS)]
    for copy in copies[::-1]:
        copy.start()
    widen(upper, upp)
    copies[3].wait()
    copies[2].wait()
    matmul_cells(upp.at[2], have.at[3], work0, have.at[2])
    copies[1].wait()
    matmul_cells(upp.at[1], work0, work1, have.at[1])
    copies[0].wait()
    matmul_cells(upp.at[0], work1, work0, have.at[0])
    pack_matrix(work0, out, 0, ROWS)


def backward_products(upper, after, chain=None):
    work = [pltpu.VMEM((MAT, LANES), F32)] * 2
    cells = pltpu.VMEM((CELLS, MAT, LANES), F32)
    across = chain is not None
    return pl.pallas_call(
        across_kernel if across else backward_kernel,
        out_shape=jax.ShapeDtypeStruct((GROUPS * ROWS, LANES), F32),
        in_specs=[whole(), anywhere()] + [anywhere()] * across,
        out_specs=whole(),
        scratch_shapes=[cells] + [cells] * across + work + [pltpu.SemaphoreType.DMA((CELLS,))] * across,
        name="across_products" if across else "backward_products",
        **params(22, 14),
    )(*((upper, after, chain) if across else (upper, after)))


def fold(parts):
    row = lax.broadcasted_iota(jnp.int32, (8, LANES), 0)
    for width in (4, 2, 1):
        lower_half = (row & width) == 0
        parts = [
            jnp.where(lower_half, one, two)
            + jnp.where(lower_half, pltpu.roll(one, 8 - width, 0), pltpu.roll(two, width, 0))
            for one, two in zip(parts[:width], parts[width:])
        ]
    return parts[0]


def matvec(block, vector):
    tiles = []
    for first in range(0, N, 8):
        parts = []
        for a in range(first, first + 8):
            product = block[a].astype(F32) * vector
            parts.append(sum(product[b : b + 8] for b in range(8, N, 8)) + product[0:8])
        tiles.append(fold(parts))
    return jnp.concatenate(tiles, axis=0)


def write_edges(delta, low, high):
    gap = jnp.zeros((LANES - 2 * N, LANES), F32)
    tiles = [jnp.concatenate([delta[2 * p], delta[2 * p + 1], gap], axis=0).T for p in range(2)]
    empty = jnp.zeros((4, LANES), F32)
    low[...] = jnp.concatenate([tiles[0][0:2], tiles[1][0:2], empty], axis=0)
    high[...] = jnp.concatenate([tiles[0][LANES - 2 :], tiles[1][LANES - 2 :], empty], axis=0)


def edges(delta):
    return pl.pallas_call(
        write_edges,
        out_shape=(jax.ShapeDtypeStruct((8, LANES), F32),) * 2,
        in_specs=[whole()],
        out_specs=(whole(),) * 2,
        name="edges",
        **params(4, 1),
    )(delta)


def source_kernel(
    rhs, delta, below, above, minus, plus, dissipation, inverse, lower, upper, *rest
):
    source, vectors, hold = rest[-3:] if len(rest) == 3 else (rest[1], rest[4], rest[3])
    lane = lax.broadcasted_iota(jnp.int32, (N, LANES), 1)
    place = lax.axis_index("surf")
    gap = jnp.zeros((LANES - 8, LANES), F32)
    before = jnp.concatenate([jnp.where(place == 0, 0.0, below[...]), gap], axis=0).T
    after = jnp.concatenate([jnp.where(place == lax.axis_size("surf") - 1, 0.0, above[...]), gap], axis=0).T
    forward = jnp.zeros((N, LANES), F32)
    for k in range(CELLS):
        centre = delta[k]
        first = k // 2 * 2
        left = before[k % 2 * N : k % 2 * N + N]
        right = after[k % 2 * N : k % 2 * N + N]

        def shifted(by):
            here = pltpu.roll(centre, by % LANES, 1)
            if by > 0:
                return jnp.where(lane < by, pltpu.roll(left, (by - 2 - first) % LANES, 1), here)
            return jnp.where(lane >= LANES + by, pltpu.roll(right, (by - first) % LANES, 1), here)

        left_one, right_one = shifted(1), shifted(-1)
        fourth = shifted(2) - 4.0 * left_one + 6.0 * centre - 4.0 * right_one + shifted(-2)
        residual = rhs[k] - dissipation[k] * fourth
        residual = residual - matvec(minus.at[k], left_one) - matvec(plus.at[k], right_one)
        value = matvec(inverse.at[k], residual)
        source[k] = value
        forward = value + matvec(lower.at[k], forward) if k else value
        hold[k] = forward
    backward = hold[CELLS - 1]
    for k in range(CELLS - 2, -1, -1):
        backward = hold[k] + matvec(upper.at[k], backward)
    gap = jnp.zeros((16, LANES), F32)
    for row, value in ((0, forward), (COLS, backward)):
        tile = jnp.concatenate([value, gap, value, gap], axis=0).T
        for i in range(COLS):
            for g in range(0, GROUPS, 8):
                start = GROUPS * i + g
                vectors[pl.ds(g, 8), row + i, :] = tile[start : start + 8]


    if len(rest) > 3:
        copy = pltpu.make_async_copy(vectors, rest[2].at[:, pl.ds(ROWS, 8), :], rest[5])
        copy.start()
        copy.wait()


def local_source(*arrays, packed=None):
    lines = jax.ShapeDtypeStruct((CELLS, N, LANES), F32)
    hold = pltpu.VMEM((CELLS, N, LANES), F32)
    if packed is None:
        return pl.pallas_call(
            source_kernel,
            out_shape=(lines, jax.ShapeDtypeStruct((GROUPS, 8, LANES), F32)),
            in_specs=[whole()] * 10,
            out_specs=(whole(), whole()),
            scratch_shapes=[hold],
            name="local_source",
            **params(16, 3),
        )(*arrays)
    return pl.pallas_call(
        source_kernel,
        out_shape=(lines, jax.ShapeDtypeStruct(packed.shape, F32)),
        in_specs=[whole()] * 10 + [pl.BlockSpec(memory_space=pl.ANY)],
        out_specs=(whole(), pl.BlockSpec(memory_space=pl.ANY)),
        scratch_shapes=[hold, pltpu.VMEM((GROUPS, 8, LANES), F32), pltpu.SemaphoreType.DMA],
        input_output_aliases={10: 1},
        name="local_source_packed",
        **params(17, 3),
    )(*arrays, packed)


def finish_kernel(incoming, source, lower, upper, delta, *rest):
    hold = rest[-1]

    def incoming_line(row):
        rows = [incoming[pl.ds(row + i, GROUPS, stride=8), :] for i in range(COLS)]
        return jnp.concatenate(rows, axis=0).T[0:N]

    value = incoming_line(0)
    for k in range(CELLS):
        value = source[k] + matvec(lower.at[k], value)
        hold[k] = value
    value = incoming_line(COLS)
    for k in range(CELLS - 1, -1, -1):
        value = hold[k] + matvec(upper.at[k], value)
        delta[k] = value
    if len(rest) > 1:
        write_edges(delta, rest[0], rest[1])


def finish(last, *arrays):
    edge = jax.ShapeDtypeStruct((8, LANES), F32)
    results = (jax.ShapeDtypeStruct((CELLS, N, LANES), F32),) + (() if last else (edge, edge))
    return pl.pallas_call(
        finish_kernel,
        out_shape=results,
        in_specs=[whole()] * 4,
        out_specs=(whole(),) * len(results),
        scratch_shapes=[pltpu.VMEM((CELLS, N, LANES), F32)],
        name="finish",
        **params(8, 1.5),
    )(*arrays)


def split(value):
    high = value.astype(BF16)
    return high, (value - high.astype(F32)).astype(BF16)


def unpack_matrix(packed, d, first, weights):
    lane = lax.broadcasted_iota(jnp.int32, (16, LANES), 1)
    extra = packed[d, pl.ds(first + 64, 8), :]
    zeros = jnp.zeros((16, LANES), F32)
    for i in range(COLS):
        block = packed[d, pl.ds(first + 16 * i, 16), :]
        turned = pltpu.roll(block, 64, 1)
        low = jnp.where(lane < 64, block, turned)
        high = jnp.where(lane < 64, turned, block)
        tail = jnp.concatenate(
            [pltpu.roll(extra, (32 - 32 * i) % LANES, 1), pltpu.roll(extra, (16 - 32 * i) % LANES, 1)], axis=0
        )
        third = jnp.where(lane < 16, pltpu.roll(block, 80, 1), jnp.where(lane < 32, pltpu.roll(block, 32, 1), tail))
        third = jnp.where(lane < 64, third, pltpu.roll(third, 64, 1))
        both = jnp.concatenate([low, high, third, zeros], axis=0)
        first_part, second_part = split(both)
        weights[pl.ds(64 * i, 64), 0:LANES] = first_part
        weights[pl.ds(64 * i, 64), LANES : 2 * LANES] = second_part


def spread(value, keep):
    wide = jnp.where(keep, jnp.concatenate([value, value], axis=1), 0.0)
    high = wide.astype(BF16).astype(F32)
    return jnp.concatenate([high, wide - high], axis=0).astype(BF16)


def kept():
    row = lax.broadcasted_iota(jnp.int32, (8, 2 * LANES), 0)
    lane = lax.broadcasted_iota(jnp.int32, (8, 2 * LANES), 1)
    return jnp.logical_and(row == lane // 64, lax.rem(lane, 64) < N)


def apply(left, weights):
    out = jnp.dot(left, weights[...], preferred_element_type=F32)
    return (out[0:8, 0:LANES] + out[8:16, 0:LANES]) + (out[0:8, LANES:] + out[8:16, LANES:])


def forward_solve_kernel(packed, vectors, out, even, odd):
    weights = (even, odd)
    keep = kept()
    base = ROWS if vectors.shape[1] > 8 else 0
    unpack_matrix(packed, 0, 0, even)

    def pair(e, state):
        for side in range(2):
            d = 2 * e + side
            unpack_matrix(packed, jnp.minimum(d + 1, GROUPS - 1), 0, weights[1 - side])
            out[d] = state
            state = vectors[d, pl.ds(base, 8), :] + apply(spread(state, keep), weights[side])
        return state

    lax.fori_loop(0, GROUPS // 2, pair, jnp.zeros((8, LANES), F32))


def backward_solve_kernel(packed, packed_b, vectors, states, out, even_g, odd_g, even_b, odd_b):
    weights_g, weights_b = (even_g, odd_g), (even_b, odd_b)
    row = lax.broadcasted_iota(jnp.int32, (8, LANES), 0)
    keep = kept()
    base = ROWS if vectors.shape[1] > 8 else 0
    last = GROUPS - 1

    def known(d, weights):
        vector = pltpu.roll(vectors[d, pl.ds(base, 8), :], COLS, 0)
        return vector + apply(spread(states[d], keep), weights)

    for e in range(2):
        unpack_matrix(packed, last - e, 0, weights_g[e])
    unpack_matrix(packed_b, last, 0, even_b)

    def pair(p, carry):
        end, ready = carry
        for side in range(2):
            e = 2 * p + side
            d = last - e
            out[d] = jnp.where(row < COLS, states[d], pltpu.roll(end, COLS, 0))
            after = jnp.maximum(d - 1, 0)
            following = known(after, weights_g[1 - side])
            unpack_matrix(packed, jnp.maximum(d - 2, 0), 0, weights_g[side])
            unpack_matrix(packed_b, after, 0, weights_b[1 - side])
            end = ready + apply(spread(end, keep), weights_b[side])
            ready = following
        return end, ready

    lax.fori_loop(0, GROUPS // 2, pair, (jnp.zeros((8, LANES), F32), known(last, even_g)))


def solve(kernel, slots, *arrays):
    return pl.pallas_call(
        kernel,
        out_shape=jax.ShapeDtypeStruct((GROUPS, 8, LANES), F32),
        in_specs=[whole()] * len(arrays),
        out_specs=whole(),
        scratch_shapes=[pltpu.VMEM((2 * LANES, 2 * LANES), BF16)] * slots,
        name=kernel.__name__,
        **params(8, 7),
    )(*arrays)


def exchange(value):
    return lax.all_to_all(value, "norm", 0, 0, tiled=True)


def shards(
    rhs, previous, minus_jac, plus_jac, dissipation, inverse_diag, lower_coupling, upper_coupling
):
    count = lax.axis_size("surf")
    up = [(i, (i + 1) % count) for i in range(count)]
    down = [((i + 1) % count, i) for i in range(count)]
    delta = previous
    low, high = edges(delta)
    backward_maps = backward_products(upper_coupling, low)
    forward_maps, chain = forward_products(lower_coupling, backward_maps)
    backward_maps = exchange(backward_maps.reshape(GROUPS, ROWS, LANES))
    forward_maps = forward_maps.reshape(GROUPS, FIRST, LANES)
    for sweep_index in range(SWEEPS):
        below = lax.ppermute(high, "surf", up)
        above = lax.ppermute(low, "surf", down)
        arrays = (
            rhs, delta, below, above, minus_jac, plus_jac, dissipation, inverse_diag, lower_coupling, upper_coupling
        )
        if sweep_index == 0:
            source, forward_maps = local_source(*arrays, packed=forward_maps)
            forward_maps = vectors = exchange(forward_maps)
            across_maps = exchange(backward_products(upper_coupling, source, chain).reshape(GROUPS, ROWS, LANES))
        else:
            source, vectors = local_source(*arrays)
            vectors = exchange(vectors)
        states = solve(forward_solve_kernel, 2, forward_maps, vectors)
        incoming = exchange(solve(backward_solve_kernel, 4, across_maps, backward_maps, vectors, states))
        last = sweep_index == SWEEPS - 1
        delta, *sides = finish(
            last, incoming.reshape(GROUPS * 8, LANES), source, lower_coupling, upper_coupling
        )
        if not last:
            low, high = sides
    return delta


def solution(mesh):
    line = P("norm", None, "surf")
    block = P("norm", None, None, "surf")
    return jax.shard_map(
        shards,
        mesh=mesh,
        in_specs=(line, line, block, block, line, block, block, block),
        out_specs=line,
        check_vma=False,
    )
```

time: 247 us -> 174 us (0.70)
  blocking collectives: 91.2 us -> 35.7 us
  Pallas kernels: 125 us -> 81.7 us
  local copies, waits for them, and re-layouts: 1.28 us -> 14 us
  starting transfers between devices: 20 us -> 30.5 us
  waiting for transfers between devices: 8.36 us -> 11.1 us
    all_to_all x4 -> x3, blocking collectives: 91.2 us -> 35.7 us  [exchange(): return lax.all_to_all(value, 'norm', 0, 0, tiled=True)]
    pallas_call x7 -> x12, Pallas kernels: 125 us -> 81.7 us  [the longest x2 30.3 us: backward_products(): pl.pallas_call(across_kernel if across else backward_kernel, out_shape=ja...]
    all_to_all x1 -> x3, starting transfers between devices: 10.2 us -> 24.3 us  [exchange(): return lax.all_to_all(value, 'norm', 0, 0, tiled=True)]
    unnamed x10 -> x54, local copies, waits for them, and re-layouts: 1.28 us -> 14 us
    all_to_all x1 -> x3, waiting for transfers between devices: 0.01 us -> 10.1 us  [exchange(): return lax.all_to_all(value, 'norm', 0, 0, tiled=True)]
    ppermute x4, waiting for transfers between devices: 8.36 us -> 1 us  [the longest x2 0.99 us: shards(): below = lax.ppermute(high, 'surf', up)]
    ppermute x4, starting transfers between devices: 9.81 us -> 6.2 us  [the longest x2 4.01 us: shards(): above = lax.ppermute(low, 'surf', down)]
  transfers between devices with their start and end apart: 5 -> 7, of which waited for: 4 -> 2; matrix products, arithmetic and copies ran while one was open for 0% -> 0% of each run, Pallas kernels for 22% -> 31%
where the time goes in v2:
time: 174 us; the launch traced here: 173 us
  Pallas kernels  81.7 us (47%)
  blocking collectives  35.7 us (21%)
  starting transfers between devices  30.5 us (18%)
  local copies, waits for them, and re-layouts  14 us (8%)
  waiting for transfers between devices  11.1 us (6%)
    all_to_all x3, blocking collectives, exchange(): return lax.all_to_all(value, 'norm', 0, 0, tiled=True)  35.7 us
    pallas_call x2, Pallas kernels, backward_products(): pl.pallas_call(across_kernel if across else backward_kernel, out_shape=ja...  30.3 us
    pallas_call x4, Pallas kernels, solve(): pl.pallas_call(kernel, out_shape=jax.ShapeDtypeStruct((GROUPS, 8, LANES),...  28.7 us
    all_to_all x3, starting transfers between devices, exchange(): return lax.all_to_all(value, 'norm', 0, 0, tiled=True)  24.3 us
    pallas_call x1, Pallas kernels, forward_products(): pl.pallas_call(forward_kernel, out_shape=(jax.ShapeDtypeStruct((GROUPS *...  14.1 us
    unnamed x54, local copies, waits for them, and re-layouts  14 us
    all_to_all x3, waiting for transfers between devices, exchange(): return lax.all_to_all(value, 'norm', 0, 0, tiled=True)  10.1 us
    ppermute x2, starting transfers between devices, shards(): above = lax.ppermute(low, 'surf', down)  4.01 us
  transfers between devices with their start and end apart: 7, of which 2 were waited for; matrix products, arithmetic and copies ran while one was open for 0% of the time, Pallas kernels for 31%

profile of v2, /device:TPU:1, one launch (start us, length us, event | category | flops | bytes accessed | tf_op | source)
XLA Modules:
  0.0 173.4 jit_solution(2878301204585465397)
XLA Ops:
  0.0 1.0 copy-done.18
  1.0 0.1 edges.1
  1.1 2.1 %collective-permute-start = (f32[8,128]{1,0:T(8,128)S(1)}, f32[8,128]{1,0:T(8,128)S(1)}, u32[]{:S(2)}, u32[]{:S(2)}) collective-permute-start(f32[8,128]{1,0:T(8,128)S(1)} %get-tuple-element.16), channel_id=1, source_target_pairs={{0,32},{32,64},{64,96},{96,0},{1,33},{33,65},{65,97},{97,1},{2,34}... | collective-permute-start | bytes 12296 | tf_op jit(solution)/shard_map/ppermute | solution.py:436
  3.3 1.3 collective-permute-start.1
  4.6 0.0 copy-done.5
  4.6 15.1 %backward_products.1.after = f32[2304,128]{1,0:T(8,128)} custom-call(bf16[4,48,48,128]{3,2,1,0:T(8,128)(2,1)S(1)} %copy-done.5, f32[8,128]{1,0:T(8,128)S(1)} %get-tuple-element.17.after), custom_call_target="tpu_custom_call" | custom-call | flops 14000000000 | tf_op jit(solution)/shard_map/backward_products/pallas_call | solution.py:157
  19.7 9.4 %all-to-all-start.1 = ((f32[32,72,128]{2,1,0:T(8,128)}), f32[32,72,128]{2,1,0:T(8,128)S(1)}, u32[]{:S(2)}, u32[]{:S(2)}) async-start(f32[32,72,128]{2,1,0:T(8,128)} %bitcast.2), calls=%async_computation.1 | async-start | bytes 2359296 | tf_op jit(solution)/shard_map/all_to_all | solution.py:420
  29.2 0.0 copy-start.9
  29.2 1.7 copy-done.9
  30.8 0.0 copy-start.10
  30.9 0.0 copy-start.14
  30.9 0.0 copy-start.16
  30.9 0.0 copy-start.19
  30.9 14.1 %forward_products.1 = (f32[2560,128]{1,0:T(8,128)S(1)}, f32[4,2304,128]{2,1,0:T(8,128)S(1)}) custom-call(bf16[4,48,48,128]{3,2,1,0:T(8,128)(2,1)S(1)} %copy-done.9, f32[2304,128]{1,0:T(8,128)} %backward_products.1.after), custom_call_target="tpu_custom_call" | custom-call | flops 12000000000 | tf_op jit(solution)/shard_map/forward_products/pallas_call | solution.py:112
  45.0 0.0 copy-start.23
  45.0 2.1 %copy-done.23 = f32[4,2304,128]{2,1,0:T(8,128)} copy-done((f32[4,2304,128]{2,1,0:T(8,128)}, f32[4,2304,128]{2,1,0:T(8,128)S(1)}, u32[]{:S(2)}) %copy-start.23) | copy-done | bytes 4718616
  47.2 0.0 collective-permute-done.below
  47.2 0.0 collective-permute-done.1.above
  47.2 0.0 copy-done
  47.2 0.0 copy-done.1
  47.2 0.0 copy-done.3
  47.2 0.0 copy-done.6
  47.2 0.0 copy-done.10
  47.2 0.0 copy-done.14
  47.2 0.0 copy-done.16
  47.2 0.0 copy-done.19
  47.2 2.8 %local_source_packed.1 = (f32[4,48,128]{2,1,0:T(8,128)S(1)}, f32[32,80,128]{2,1,0:T(8,128)S(1)}) custom-call(f32[4,48,128]{2,1,0:T(8,128)S(1)} %copy-done.14, f32[4,48,128]{2,1,0:T(8,128)S(1)} %copy-done.19, f32[8,128]{1,0:T(8,128)S(1)} %collective-permute-done.below, f32[8,128]{1,0:T(8,128)S(1)} %collective-permute-done.1.above, ...), custom_call_target="tpu_custom_call", output_to_operand_aliasing={{1}: (10, {})} | custom-call | flops 3000000000 | tf_op jit(solution)/shard_map/local_source_packed/pallas_call | solution.py:271
  50.0 0.0 copy-start.12
  50.0 1.0 copy-done.12
  51.1 0.6 copy-done.20
  51.7 0.0 all-to-all-done.1.packed_b
  51.7 7.4 %all-to-all-start.2 = ((f32[32,80,128]{2,1,0:T(8,128)}), f32[32,80,128]{2,1,0:T(8,128)}, u32[]{:S(2)}, u32[]{:S(2)}) async-start(f32[32,80,128]{2,1,0:T(8,128)} %copy-done.12), calls=%async_computation.2 | async-start | bytes 2621440 | tf_op jit(solution)/shard_map/all_to_all | solution.py:420
  59.2 0.0 copy-start.7
  59.2 1.7 copy-done.7
  60.8 0.9 copy-done.21
  61.7 2.3 %copy-done.24 = f32[4,2304,128]{2,1,0:T(8,128)S(1)} copy-done((f32[4,2304,128]{2,1,0:T(8,128)S(1)}, f32[4,2304,128]{2,1,0:T(8,128)}, u32[]{:S(2)}) %copy-start.24) | copy-done | bytes 4718616
  64.1 15.2 %across_products.1 = f32[2304,128]{1,0:T(8,128)S(1)} custom-call(bf16[4,48,48,128]{3,2,1,0:T(8,128)(2,1)S(1)} %copy-done.7, f32[4,48,128]{2,1,0:T(8,128)S(1)} %copy-done.21, f32[4,2304,128]{2,1,0:T(8,128)S(1)} %copy-done.24), custom_call_target="tpu_custom_call" | custom-call | flops 14000000000 | tf_op jit(solution)/shard_map/across_products/pallas_call | solution.py:157
  79.3 0.0 copy-start.13
  79.3 1.0 copy-done.13
  80.3 0.0 all-to-all-done.2.packed.vectors
  80.3 7.4 %all-to-all-start = ((f32[32,72,128]{2,1,0:T(8,128)}), f32[32,72,128]{2,1,0:T(8,128)}, u32[]{:S(2)}, u32[]{:S(2)}) async-start(f32[32,72,128]{2,1,0:T(8,128)} %bitcast.6), calls=%async_computation | async-start | bytes 2359296 | tf_op jit(solution)/shard_map/all_to_all | solution.py:420
  87.7 7.0 %forward_solve_kernel.2.states = f32[32,8,128]{2,1,0:T(8,128)S(1)} custom-call(f32[32,80,128]{2,1,0:T(8,128)} %all-to-all-done.2.packed.vectors, f32[32,80,128]{2,1,0:T(8,128)} %all-to-all-done.2.packed.vectors), custom_call_target="tpu_custom_call" | custom-call | flops 7000000000 | tf_op jit(solution)/shard_map/forward_solve_kernel/pallas_call | solution.py:408
  94.7 0.7 copy-done.25
  95.4 10.1 %all-to-all-done.packed = f32[32,72,128]{2,1,0:T(8,128)} async-done(((f32[32,72,128]{2,1,0:T(8,128)}), f32[32,72,128]{2,1,0:T(8,128)}, u32[]{:S(2)}, u32[]{:S(2)}) %all-to-all-start) | async-done | bytes 1179680 | tf_op jit(solution)/shard_map/all_to_all | solution.py:420
  105.5 0.9 copy-done.26
  106.4 7.8 %backward_solve_kernel.2 = f32[32,8,128]{2,1,0:T(8,128)S(1)} custom-call(f32[32,72,128]{2,1,0:T(8,128)} %all-to-all-done.packed, f32[32,72,128]{2,1,0:T(8,128)S(1)} %all-to-all-done.1.packed_b, f32[32,80,128]{2,1,0:T(8,128)} %all-to-all-done.2.packed.vectors, f32[32,8,128]{2,1,0:T(8,128)S(1)} %copy-done.26), custom_call_target="tpu_custom_call" | custom-call | flops 7000000000 | tf_op jit(solution)/shard_map/backward_solve_kernel/pallas_call | solution.py:408
  114.2 12.0 %all_to_all.30 = f32[32,8,128]{2,1,0:T(8,128)S(1)} all-to-all(f32[32,8,128]{2,1,0:T(8,128)S(1)} %backward_solve_kernel.2), channel_id=1, replica_groups=mesh['surf'=4,'norm'=32] {'norm'}, dimensions={0} | all-to-all | bytes 262144 | tf_op jit(solution)/shard_map/all_to_all | solution.py:420
  126.2 0.0 copy-done.8
  126.3 0.0 copy-start.2
  126.3 0.0 copy-start.4
  126.3 0.0 copy-start.15
  126.3 0.0 copy-start.17
  126.3 1.2 finish.2
  127.5 0.1 collective-permute-start.2
  127.6 2.7 %collective-permute-start.3 = (f32[8,128]{1,0:T(8,128)S(1)}, f32[8,128]{1,0:T(8,128)S(1)}, u32[]{:S(2)}, u32[]{:S(2)}) collective-permute-start(f32[8,128]{1,0:T(8,128)S(1)} %get-tuple-element.24), channel_id=1, source_target_pairs={{32,0},{64,32},{96,64},{0,96},{33,1},{65,33},{97,65},{1,97},{34,2}... | collective-permute-start | bytes 12296 | tf_op jit(solution)/shard_map/ppermute | solution.py:437
  130.3 1.0 collective-permute-done.2.below
  131.3 0.0 collective-permute-done.3.above
  131.3 0.0 copy-done.2
  131.3 2.8 %local_source.1 = (f32[4,48,128]{2,1,0:T(8,128)S(1)}, f32[32,8,128]{2,1,0:T(8,128)S(1)}) custom-call(f32[4,48,128]{2,1,0:T(8,128)S(1)} %copy-done.15, f32[4,48,128]{2,1,0:T(8,128)S(1)} %get-tuple-element.22.delta, f32[8,128]{1,0:T(8,128)S(1)} %collective-permute-done.2.below, f32[8,128]{1,0:T(8,128)S(1)} %collective-permute-done.3.above, ...), custom_call_target="tpu_custom_call" | custom-call | flops 3000000000 | tf_op jit(solution)/shard_map/local_source/pallas_call | solution.py:262
  134.1 12.4 %all_to_all.31.vectors = f32[32,8,128]{2,1,0:T(8,128)S(1)} all-to-all(f32[32,8,128]{2,1,0:T(8,128)S(1)} %get-tuple-element.25), channel_id=1, replica_groups=mesh['surf'=4,'norm'=32] {'norm'}, dimensions={0} | all-to-all | bytes 262144 | tf_op jit(solution)/shard_map/all_to_all | solution.py:420
  146.5 6.5 %forward_solve_kernel.3.states = f32[32,8,128]{2,1,0:T(8,128)S(1)} custom-call(f32[32,80,128]{2,1,0:T(8,128)} %all-to-all-done.2.packed.vectors, f32[32,8,128]{2,1,0:T(8,128)S(1)} %all_to_all.31.vectors), custom_call_target="tpu_custom_call" | custom-call | flops 7000000000 | tf_op jit(solution)/shard_map/forward_solve_kernel/pallas_call | solution.py:408
  153.0 7.3 %backward_solve_kernel.3 = f32[32,8,128]{2,1,0:T(8,128)S(1)} custom-call(f32[32,72,128]{2,1,0:T(8,128)} %all-to-all-done.packed, f32[32,72,128]{2,1,0:T(8,128)S(1)} %all-to-all-done.1.packed_b, f32[32,8,128]{2,1,0:T(8,128)S(1)} %all_to_all.31.vectors, f32[32,8,128]{2,1,0:T(8,128)S(1)} %forward_solve_kernel.3.states), custom_call_target="tpu_custom_call" | custom-call | flops 7000000000 | tf_op jit(solution)/shard_map/backward_solve_kernel/pallas_call | solution.py:408
  160.3 11.3 %all_to_all.32 = f32[32,8,128]{2,1,0:T(8,128)S(1)} all-to-all(f32[32,8,128]{2,1,0:T(8,128)S(1)} %backward_solve_kernel.3), channel_id=1, replica_groups=mesh['surf'=4,'norm'=32] {'norm'}, dimensions={0} | all-to-all | bytes 262144 | tf_op jit(solution)/shard_map/all_to_all | solution.py:420
  171.6 1.8 %finish.3 = f32[4,48,128]{2,1,0:T(8,128)} custom-call(f32[256,128]{1,0:T(8,128)S(1)} %bitcast.8, f32[4,48,128]{2,1,0:T(8,128)S(1)} %get-tuple-element.26.source, bf16[4,48,48,128]{3,2,1,0:T(8,128)(2,1)S(1)} %copy-done.11, bf16[4,48,48,128]{3,2,1,0:T(8,128)(2,1)S(1)} %copy-done.8), custom_call_target="tpu_custom_call" | custom-call | flops 1500000000 | tf_op jit(solution)/shard_map/finish/pallas_call | solution.py:305
  (19 shorter events, 0.0 us)
Async XLA Ops:
  0.0 4.6 %copy-start.5 = (bf16[4,48,48,128]{3,2,1,0:T(8,128)(2,1)S(1)}, bf16[4,48,48,128]{3,2,1,0:T(8,128)(2,1)}, u32[]{:S(2)}) copy-start(bf16[4,48,48,128]{3,2,1,0:T(8,128)(2,1)} %upper.11) | copy-start | bytes 7077892
  0.0 1.0 copy-start.18
  1.1 46.0 %collective-permute-start = (f32[8,128]{1,0:T(8,128)S(1)}, f32[8,128]{1,0:T(8,128)S(1)}, u32[]{:S(2)}, u32[]{:S(2)}) collective-permute-start(f32[8,128]{1,0:T(8,128)S(1)} %get-tuple-element.16), channel_id=1, source_target_pairs={{0,32},{32,64},{64,96},{96,0},{1,33},{33,65},{65,97},{97,1},{2,34}... | collective-permute-start | bytes 12296 | tf_op jit(solution)/shard_map/ppermute | solution.py:436
  3.3 43.9 %collective-permute-start.1 = (f32[8,128]{1,0:T(8,128)S(1)}, f32[8,128]{1,0:T(8,128)S(1)}, u32[]{:S(2)}, u32[]{:S(2)}) collective-permute-start(f32[8,128]{1,0:T(8,128)S(1)} %get-tuple-element.17.after), channel_id=1, source_target_pairs={{32,0},{64,32},{96,64},{0,96},{33,1},{65,33},{97,65},{1,97},{34,2}... | collective-permute-start | bytes 12296 | tf_op jit(solution)/shard_map/ppermute | solution.py:437
  19.7 32.0 %all-to-all-start.1 = ((f32[32,72,128]{2,1,0:T(8,128)}), f32[32,72,128]{2,1,0:T(8,128)S(1)}, u32[]{:S(2)}, u32[]{:S(2)}) async-start(f32[32,72,128]{2,1,0:T(8,128)} %bitcast.2), calls=%async_computation.1 | async-start | bytes 2359296 | tf_op jit(solution)/shard_map/all_to_all | solution.py:420
  29.2 1.7 copy-start.9
  30.8 16.3 %copy-start = (bf16[4,48,48,128]{3,2,1,0:T(8,128)(2,1)S(1)}, bf16[4,48,48,128]{3,2,1,0:T(8,128)(2,1)}, u32[]{:S(2)}) copy-start(bf16[4,48,48,128]{3,2,1,0:T(8,128)(2,1)} %minus.3) | copy-start | bytes 7077892
  30.8 16.3 %copy-start.1 = (bf16[4,48,48,128]{3,2,1,0:T(8,128)(2,1)S(1)}, bf16[4,48,48,128]{3,2,1,0:T(8,128)(2,1)}, u32[]{:S(2)}) copy-start(bf16[4,48,48,128]{3,2,1,0:T(8,128)(2,1)} %plus.3) | copy-start | bytes 7077892
  30.8 16.3 %copy-start.3 = (bf16[4,48,48,128]{3,2,1,0:T(8,128)(2,1)S(1)}, bf16[4,48,48,128]{3,2,1,0:T(8,128)(2,1)}, u32[]{:S(2)}) copy-start(bf16[4,48,48,128]{3,2,1,0:T(8,128)(2,1)} %inverse.3) | copy-start | bytes 7077892
  30.8 16.4 %copy-start.6 = (bf16[4,48,48,128]{3,2,1,0:T(8,128)(2,1)S(1)}, bf16[4,48,48,128]{3,2,1,0:T(8,128)(2,1)}, u32[]{:S(2)}) copy-start(bf16[4,48,48,128]{3,2,1,0:T(8,128)(2,1)} %upper.11) | copy-start | bytes 7077892
  30.8 16.4 %copy-start.10 = (bf16[4,48,48,128]{3,2,1,0:T(8,128)(2,1)S(1)}, bf16[4,48,48,128]{3,2,1,0:T(8,128)(2,1)}, u32[]{:S(2)}) copy-start(bf16[4,48,48,128]{3,2,1,0:T(8,128)(2,1)} %lower.9) | copy-start | bytes 7077892
  30.9 16.4 %copy-start.14 = (f32[4,48,128]{2,1,0:T(8,128)S(1)}, f32[4,48,128]{2,1,0:T(8,128)}, u32[]{:S(2)}) copy-start(f32[4,48,128]{2,1,0:T(8,128)} %rhs.3) | copy-start | bytes 294916
  30.9 16.4 %copy-start.16 = (f32[4,48,128]{2,1,0:T(8,128)S(1)}, f32[4,48,128]{2,1,0:T(8,128)}, u32[]{:S(2)}) copy-start(f32[4,48,128]{2,1,0:T(8,128)} %dissipation.3) | copy-start | bytes 294916
  30.9 16.4 %copy-start.19 = (f32[4,48,128]{2,1,0:T(8,128)S(1)}, f32[4,48,128]{2,1,0:T(8,128)}, u32[]{:S(2)}) copy-start(f32[4,48,128]{2,1,0:T(8,128)} %delta.3) | copy-start | bytes 294916
  45.0 2.1 %copy-start.23 = (f32[4,2304,128]{2,1,0:T(8,128)}, f32[4,2304,128]{2,1,0:T(8,128)S(1)}, u32[]{:S(2)}) copy-start(f32[4,2304,128]{2,1,0:T(8,128)S(1)} %get-tuple-element.20.chain) | copy-start | bytes 14155780
  50.0 1.1 copy-start.12
  51.1 0.6 copy-start.20
  51.7 28.6 %all-to-all-start.2 = ((f32[32,80,128]{2,1,0:T(8,128)}), f32[32,80,128]{2,1,0:T(8,128)}, u32[]{:S(2)}, u32[]{:S(2)}) async-start(f32[32,80,128]{2,1,0:T(8,128)} %copy-done.12), calls=%async_computation.2 | async-start | bytes 2621440 | tf_op jit(solution)/shard_map/all_to_all | solution.py:420
  59.2 1.7 copy-start.7
  60.8 0.9 copy-start.21
  61.7 2.3 %copy-start.24 = (f32[4,2304,128]{2,1,0:T(8,128)S(1)}, f32[4,2304,128]{2,1,0:T(8,128)}, u32[]{:S(2)}) copy-start(f32[4,2304,128]{2,1,0:T(8,128)} %copy-done.23) | copy-start | bytes 14155780
  79.3 1.0 copy-start.13
  80.3 25.2 %all-to-all-start = ((f32[32,72,128]{2,1,0:T(8,128)}), f32[32,72,128]{2,1,0:T(8,128)}, u32[]{:S(2)}, u32[]{:S(2)}) async-start(f32[32,72,128]{2,1,0:T(8,128)} %bitcast.6), calls=%async_computation | async-start | bytes 2359296 | tf_op jit(solution)/shard_map/all_to_all | solution.py:420
  94.7 0.7 copy-start.25
  105.5 0.9 copy-start.26
  106.4 19.9 %copy-start.8 = (bf16[4,48,48,128]{3,2,1,0:T(8,128)(2,1)S(1)}, bf16[4,48,48,128]{3,2,1,0:T(8,128)(2,1)}, u32[]{:S(2)}) copy-start(bf16[4,48,48,128]{3,2,1,0:T(8,128)(2,1)} %upper.11) | copy-start | bytes 7077892
  106.4 19.9 %copy-start.11 = (bf16[4,48,48,128]{3,2,1,0:T(8,128)(2,1)S(1)}, bf16[4,48,48,128]{3,2,1,0:T(8,128)(2,1)}, u32[]{:S(2)}) copy-start(bf16[4,48,48,128]{3,2,1,0:T(8,128)(2,1)} %lower.9) | copy-start | bytes 7077892
  106.4 19.9 %copy-start.22 = (f32[4,48,128]{2,1,0:T(8,128)S(1)}, f32[4,48,128]{2,1,0:T(8,128)}, u32[]{:S(2)}) copy-start(f32[4,48,128]{2,1,0:T(8,128)} %copy-done.20) | copy-start | bytes 294916
  126.3 5.0 %copy-start.2 = (bf16[4,48,48,128]{3,2,1,0:T(8,128)(2,1)S(1)}, bf16[4,48,48,128]{3,2,1,0:T(8,128)(2,1)}, u32[]{:S(2)}) copy-start(bf16[4,48,48,128]{3,2,1,0:T(8,128)(2,1)} %plus.3) | copy-start | bytes 7077892
  126.3 5.0 %copy-start.4 = (bf16[4,48,48,128]{3,2,1,0:T(8,128)(2,1)S(1)}, bf16[4,48,48,128]{3,2,1,0:T(8,128)(2,1)}, u32[]{:S(2)}) copy-start(bf16[4,48,48,128]{3,2,1,0:T(8,128)(2,1)} %inverse.3) | copy-start | bytes 7077892
  126.3 5.0 %copy-start.15 = (f32[4,48,128]{2,1,0:T(8,128)S(1)}, f32[4,48,128]{2,1,0:T(8,128)}, u32[]{:S(2)}) copy-start(f32[4,48,128]{2,1,0:T(8,128)} %rhs.3) | copy-start | bytes 294916
  126.3 5.0 %copy-start.17 = (f32[4,48,128]{2,1,0:T(8,128)S(1)}, f32[4,48,128]{2,1,0:T(8,128)}, u32[]{:S(2)}) copy-start(f32[4,48,128]{2,1,0:T(8,128)} %dissipation.3) | copy-start | bytes 294916
  127.5 3.7 %collective-permute-start.2 = (f32[8,128]{1,0:T(8,128)S(1)}, f32[8,128]{1,0:T(8,128)S(1)}, u32[]{:S(2)}, u32[]{:S(2)}) collective-permute-start(f32[8,128]{1,0:T(8,128)S(1)} %get-tuple-element.23), channel_id=1, source_target_pairs={{0,32},{32,64},{64,96},{96,0},{1,33},{33,65},{65,97},{97,1},{2,34}... | collective-permute-start | bytes 12296 | tf_op jit(solution)/shard_map/ppermute | solution.py:436
  127.6 3.7 %collective-permute-start.3 = (f32[8,128]{1,0:T(8,128)S(1)}, f32[8,128]{1,0:T(8,128)S(1)}, u32[]{:S(2)}, u32[]{:S(2)}) collective-permute-start(f32[8,128]{1,0:T(8,128)S(1)} %get-tuple-element.24), channel_id=1, source_target_pairs={{32,0},{64,32},{96,64},{0,96},{33,1},{65,33},{97,65},{1,97},{34,2}... | collective-permute-start | bytes 12296 | tf_op jit(solution)/shard_map/ppermute | solution.py:437

commit v3 on v2

--- a/solution.py
+++ b/solution.py
@@ -16,6 +16,7 @@
 COLS = LANES // GROUPS
 ROWS = 72
 FIRST = ROWS + 8
+ROOM = 60
 F32 = jnp.float32
 BF16 = jnp.bfloat16
 
@@ -51,7 +52,7 @@
     lax.fori_loop(0, N // 4, block, 0)
 
 
-def pack_matrix(mat, out, first, pitch):
+def pack_matrix(mat, out, first):
     def column(c, lo, count):
         return mat[pl.ds(c + lo * N, count, stride=N), :]
 
@@ -60,7 +61,8 @@
             [column(r, 0, 48), column(32 + r, 0, 16), column(16 + r, 0, 48), column(32 + r, 16, 16)], axis=0
         ).T
         for i in range(COLS):
-            out[pl.ds(first + i * 16 + r, GROUPS, stride=pitch), :] = tile[GROUPS * i : GROUPS * (i + 1)]
+            for g in range(0, GROUPS, 8):
+                out[pl.ds(g, 8), first + i * 16 + r, :] = tile[GROUPS * i + g : GROUPS * i + g + 8]
         return carry
 
     lax.fori_loop(0, 16, main, 0, unroll=4)
@@ -69,16 +71,22 @@
         tile = jnp.concatenate(
             [column(32 + r, 32, 16), column(40 + r, 32, 16), jnp.zeros((96, LANES), F32)], axis=0
         ).T
-        out[pl.ds(first + 64 + r, GROUPS, stride=pitch), :] = jnp.concatenate(
-            [tile[GROUPS * i : GROUPS * (i + 1), 0:32] for i in range(COLS)], axis=1
-        )
+        line = jnp.concatenate([tile[GROUPS * i : GROUPS * (i + 1), 0:32] for i in range(COLS)], axis=1)
+        for g in range(0, GROUPS, 8):
+            out[pl.ds(g, 8), first + 64 + r, :] = line[g : g + 8]
         return carry
 
     lax.fori_loop(0, 8, rest, 0, unroll=4)
 
 
-def widen(narrow, wide):
-    for k in range(CELLS):
+def in_hbm():
+    return pl.BlockSpec(memory_space=pltpu.HBM)
+
+
+def widen(narrow, wide, copies, cells):
+    for k in cells:
+        copies[k].wait()
+
         def row(r, carry):
             wide[k, pl.ds(pl.multiple_of(r * N, 16), N), :] = narrow[k, r].astype(F32)
             return carry
@@ -86,82 +94,137 @@
         lax.fori_loop(0, N, row, 0, unroll=4)
 
 
-def anywhere():
-    return pl.BlockSpec(memory_space=pl.ANY)
-
-
-def forward_kernel(lower, after, out, chain, low, work, sems):
-    widen(lower, low)
-    copies = []
+def fetch(source, target, sems, order):
+    copies = {k: pltpu.make_async_copy(source.at[k], target.at[k], sems.at[k]) for k in order}
+    for k in order:
+        copies[k].start()
+    return copies
+
+
+def write_out(packed, out, rows, sem):
+    copy = pltpu.make_async_copy(packed, out.at[:, pl.ds(0, rows), :] if rows < out.shape[1] else out, sem)
+    copy.start()
+    copy.wait()
+
+
+def forward_kernel(
+    rhs, delta, below, above, minus, plus, dissipation, inverse, lower, upper, after,
+    out, source, chain,
+    narrow, low, work, packed, sems, chain_sems, out_sem, blocks, block_sems, hold, vectors,
+):
+    copies = fetch(lower, narrow, sems, (0, 1, 2, 3))
+    others = [
+        pltpu.make_async_copy(array, blocks.at[which], block_sems.at[which])
+        for which, array in enumerate((minus, plus, inverse, upper))
+    ]
+    for copy in others:
+        copy.start()
+    kept = []
 
     def keep(k, ref):
-        copies.append(pltpu.make_async_copy(ref, chain.at[k], sems.at[k]))
-        copies[-1].start()
-
+        kept.append(pltpu.make_async_copy(ref, chain.at[k], chain_sems.at[k]))
+        kept[-1].start()
+
+    widen(narrow, low, copies, (0, 1))
     keep(0, low.at[0])
     for k in range(1, CELLS):
         before = low.at[0] if k == 1 else work.at[k - 2]
+        if k > 1:
+            widen(narrow, low, copies, (k,))
         matmul_cells(low.at[k], before, work.at[k - 1])
         keep(k, work.at[k - 1])
-    pack_matrix(work.at[CELLS - 2], out, 0, FIRST)
-    for copy in copies:
+    pack_matrix(work.at[CELLS - 2], packed, 0)
+    copy = pltpu.make_async_copy(packed, out.at[:, pl.ds(0, ROWS), :], out_sem)
+    copy.start()
+    for other in others:
+        other.wait()
+    source_kernel(
+        rhs, delta, below, above, blocks.at[0], blocks.at[1], dissipation, blocks.at[2], narrow, blocks.at[3],
+        source, vectors, hold,
+    )
+    copy.wait()
+    copy = pltpu.make_async_copy(vectors, out.at[:, pl.ds(ROWS, 8), :], out_sem)
+    copy.start()
+    copy.wait()
+    for copy in kept:
         copy.wait()
 
 
-def forward_products(lower, after):
+def product_scratch(works):
+    return [
+        pltpu.VMEM((CELLS, N, N, LANES), BF16),
+        pltpu.VMEM((CELLS, MAT, LANES), F32),
+        pltpu.VMEM((works, MAT, LANES), F32),
+        pltpu.VMEM((GROUPS, ROWS, LANES), F32),
+        pltpu.SemaphoreType.DMA((CELLS,)),
+        pltpu.SemaphoreType.DMA((CELLS,)),
+        pltpu.SemaphoreType.DMA,
+    ]
+
+
+def forward_products(*arrays):
+    lines = (CELLS, N, LANES)
     return pl.pallas_call(
         forward_kernel,
         out_shape=(
-            jax.ShapeDtypeStruct((GROUPS * FIRST, LANES), F32),
+            jax.ShapeDtypeStruct((GROUPS, FIRST, LANES), F32),
+            jax.ShapeDtypeStruct(lines, F32),
             jax.ShapeDtypeStruct((CELLS, MAT, LANES), F32),
         ),
-        in_specs=[whole(), anywhere()],
-        out_specs=(whole(), anywhere()),
-        scratch_shapes=[
-            pltpu.VMEM((CELLS, MAT, LANES), F32),
-            pltpu.VMEM((CELLS - 1, MAT, LANES), F32),
-            pltpu.SemaphoreType.DMA((CELLS,)),
+        in_specs=[whole()] * 4 + [in_hbm()] * 2 + [whole()] + [in_hbm()] * 4,
+        out_specs=(in_hbm(), whole(), in_hbm()),
+        scratch_shapes=product_scratch(3)
+        + [
+            pltpu.VMEM((4, CELLS, N, N, LANES), BF16),
+            pltpu.SemaphoreType.DMA((4,)),
+            pltpu.VMEM(lines, F32),
+            pltpu.VMEM((GROUPS, 8, LANES), F32),
         ],
         name="forward_products",
-        **params(20, 12),
-    )(lower, after)
-
-
-def backward_kernel(upper, after, out, upp, work0, work1):
-    widen(upper, upp)
-    matmul_cells(upp.at[2], upp.at[3], work0)
-    matmul_cells(upp.at[1], work0, work1)
-    matmul_cells(upp.at[0], work1, work0)
-    pack_matrix(work0, out, 0, ROWS)
-
-
-def across_kernel(upper, after, chain, out, upp, have, work0, work1, sems):
-    copies = [pltpu.make_async_copy(chain.at[k], have.at[k], sems.at[k]) for k in range(CELLS)]
-    for copy in copies[::-1]:
-        copy.start()
-    widen(upper, upp)
-    copies[3].wait()
-    copies[2].wait()
-    matmul_cells(upp.at[2], have.at[3], work0, have.at[2])
-    copies[1].wait()
-    matmul_cells(upp.at[1], work0, work1, have.at[1])
-    copies[0].wait()
-    matmul_cells(upp.at[0], work1, work0, have.at[0])
-    pack_matrix(work0, out, 0, ROWS)
+        **params(ROOM - 5, 17),
+    )(*arrays)
+
+
+def backward_kernel(upper, after, out, narrow, upp, work, packed, sems, more_sems, out_sem):
+    copies = fetch(upper, narrow, sems, (3, 2, 1, 0))
+    widen(narrow, upp, copies, (3, 2))
+    matmul_cells(upp.at[2], upp.at[3], work.at[0])
+    widen(narrow, upp, copies, (1,))
+    matmul_cells(upp.at[1], work.at[0], work.at[1])
+    widen(narrow, upp, copies, (0,))
+    matmul_cells(upp.at[0], work.at[1], work.at[0])
+    pack_matrix(work.at[0], packed, 0)
+    write_out(packed, out, ROWS, out_sem)
+
+
+def across_kernel(upper, after, chain, out, narrow, upp, work, packed, sems, chain_sems, out_sem, have):
+    copies = fetch(upper, narrow, sems, (2,))
+    chains = fetch(chain, have, chain_sems, (3, 2, 1, 0))
+    copies.update(fetch(upper, narrow, sems, (1, 0)))
+    widen(narrow, upp, copies, (2,))
+    chains[3].wait()
+    chains[2].wait()
+    matmul_cells(upp.at[2], have.at[3], work.at[0], have.at[2])
+    widen(narrow, upp, copies, (1,))
+    chains[1].wait()
+    matmul_cells(upp.at[1], work.at[0], work.at[1], have.at[1])
+    widen(narrow, upp, copies, (0,))
+    chains[0].wait()
+    matmul_cells(upp.at[0], work.at[1], work.at[0], have.at[0])
+    pack_matrix(work.at[0], packed, 0)
+    write_out(packed, out, ROWS, out_sem)
 
 
 def backward_products(upper, after, chain=None):
-    work = [pltpu.VMEM((MAT, LANES), F32)] * 2
-    cells = pltpu.VMEM((CELLS, MAT, LANES), F32)
     across = chain is not None
     return pl.pallas_call(
         across_kernel if across else backward_kernel,
-        out_shape=jax.ShapeDtypeStruct((GROUPS * ROWS, LANES), F32),
-        in_specs=[whole(), anywhere()] + [anywhere()] * across,
-        out_specs=whole(),
-        scratch_shapes=[cells] + [cells] * across + work + [pltpu.SemaphoreType.DMA((CELLS,))] * across,
+        out_shape=jax.ShapeDtypeStruct((GROUPS, ROWS, LANES), F32),
+        in_specs=[in_hbm()] * (3 if across else 2),
+        out_specs=in_hbm(),
+        scratch_shapes=product_scratch(2) + [pltpu.VMEM((CELLS, MAT, LANES), F32)] * across,
         name="across_products" if across else "backward_products",
-        **params(22, 14),
+        **params(ROOM, 15),
     )(*((upper, after, chain) if across else (upper, after)))
 
 
@@ -208,9 +271,9 @@
 
 
 def source_kernel(
-    rhs, delta, below, above, minus, plus, dissipation, inverse, lower, upper, *rest
+    rhs, delta, below, above, minus, plus, dissipation, inverse, lower, upper,
+    source, vectors, hold,
 ):
-    source, vectors, hold = rest[-3:] if len(rest) == 3 else (rest[1], rest[4], rest[3])
     lane = lax.broadcasted_iota(jnp.int32, (N, LANES), 1)
     place = lax.axis_index("surf")
     gap = jnp.zeros((LANES - 8, LANES), F32)
@@ -249,35 +312,17 @@
                 vectors[pl.ds(g, 8), row + i, :] = tile[start : start + 8]
 
 
-    if len(rest) > 3:
-        copy = pltpu.make_async_copy(vectors, rest[2].at[:, pl.ds(ROWS, 8), :], rest[5])
-        copy.start()
-        copy.wait()
-
-
-def local_source(*arrays, packed=None):
-    lines = jax.ShapeDtypeStruct((CELLS, N, LANES), F32)
-    hold = pltpu.VMEM((CELLS, N, LANES), F32)
-    if packed is None:
-        return pl.pallas_call(
-            source_kernel,
-            out_shape=(lines, jax.ShapeDtypeStruct((GROUPS, 8, LANES), F32)),
-            in_specs=[whole()] * 10,
-            out_specs=(whole(), whole()),
-            scratch_shapes=[hold],
-            name="local_source",
-            **params(16, 3),
-        )(*arrays)
+def local_source(*arrays):
+    lines = (CELLS, N, LANES)
     return pl.pallas_call(
         source_kernel,
-        out_shape=(lines, jax.ShapeDtypeStruct(packed.shape, F32)),
-        in_specs=[whole()] * 10 + [pl.BlockSpec(memory_space=pl.ANY)],
-        out_specs=(whole(), pl.BlockSpec(memory_space=pl.ANY)),
-        scratch_shapes=[hold, pltpu.VMEM((GROUPS, 8, LANES), F32), pltpu.SemaphoreType.DMA],
-        input_output_aliases={10: 1},
-        name="local_source_packed",
-        **params(17, 3),
-    )(*arrays, packed)
+        out_shape=(jax.ShapeDtypeStruct(lines, F32), jax.ShapeDtypeStruct((GROUPS, 8, LANES), F32)),
+        in_specs=[whole()] * 10,
+        out_specs=(whole(), whole()),
+        scratch_shapes=[pltpu.VMEM(lines, F32)],
+        name="local_source",
+        **params(16, 3),
+    )(*arrays)
 
 
 def finish_kernel(incoming, source, lower, upper, delta, *rest):
@@ -321,7 +366,6 @@
 def unpack_matrix(packed, d, first, weights):
     lane = lax.broadcasted_iota(jnp.int32, (16, LANES), 1)
     extra = packed[d, pl.ds(first + 64, 8), :]
-    zeros = jnp.zeros((16, LANES), F32)
     for i in range(COLS):
         block = packed[d, pl.ds(first + 16 * i, 16), :]
         turned = pltpu.roll(block, 64, 1)
@@ -332,10 +376,16 @@
         )
         third = jnp.where(lane < 16, pltpu.roll(block, 80, 1), jnp.where(lane < 32, pltpu.roll(block, 32, 1), tail))
         third = jnp.where(lane < 64, third, pltpu.roll(third, 64, 1))
-        both = jnp.concatenate([low, high, third, zeros], axis=0)
+        both = jnp.concatenate([low, high, third], axis=0)
         first_part, second_part = split(both)
-        weights[pl.ds(64 * i, 64), 0:LANES] = first_part
-        weights[pl.ds(64 * i, 64), LANES : 2 * LANES] = second_part
+        weights[pl.ds(64 * i, N), 0:LANES] = first_part
+        weights[pl.ds(64 * i, N), LANES : 2 * LANES] = second_part
+
+
+def clear_gaps(*weights):
+    for ref in weights:
+        for i in range(COLS):
+            ref[pl.ds(64 * i + N, 64 - N), :] = jnp.zeros((64 - N, 2 * LANES), BF16)
 
 
 def spread(value, keep):
@@ -359,30 +409,34 @@
     weights = (even, odd)
     keep = kept()
     base = ROWS if vectors.shape[1] > 8 else 0
+    clear_gaps(even, odd)
     unpack_matrix(packed, 0, 0, even)
 
     def pair(e, state):
         for side in range(2):
             d = 2 * e + side
+            product = apply(spread(state, keep), weights[side])
+            vector = vectors[d, pl.ds(base, 8), :]
+            out[d, 0:8] = state
+            out[d, 8:16] = vector
             unpack_matrix(packed, jnp.minimum(d + 1, GROUPS - 1), 0, weights[1 - side])
-            out[d] = state
-            state = vectors[d, pl.ds(base, 8), :] + apply(spread(state, keep), weights[side])
+            state = vector + product
         return state
 
     lax.fori_loop(0, GROUPS // 2, pair, jnp.zeros((8, LANES), F32))
 
 
-def backward_solve_kernel(packed, packed_b, vectors, states, out, even_g, odd_g, even_b, odd_b):
+def backward_solve_kernel(packed, packed_b, states, out, even_g, odd_g, even_b, odd_b):
     weights_g, weights_b = (even_g, odd_g), (even_b, odd_b)
     row = lax.broadcasted_iota(jnp.int32, (8, LANES), 0)
     keep = kept()
-    base = ROWS if vectors.shape[1] > 8 else 0
     last = GROUPS - 1
 
     def known(d, weights):
-        vector = pltpu.roll(vectors[d, pl.ds(base, 8), :], COLS, 0)
-        return vector + apply(spread(states[d], keep), weights)
-
+        vector = pltpu.roll(states[d, 8:16], COLS, 0)
+        return vector + apply(spread(states[d, 0:8], keep), weights)
+
+    clear_gaps(even_g, odd_g, even_b, odd_b)
     for e in range(2):
         unpack_matrix(packed, last - e, 0, weights_g[e])
     unpack_matrix(packed_b, last, 0, even_b)
@@ -392,27 +446,27 @@
         for side in range(2):
             e = 2 * p + side
             d = last - e
-            out[d] = jnp.where(row < COLS, states[d], pltpu.roll(end, COLS, 0))
+            product = apply(spread(end, keep), weights_b[side])
+            out[d] = jnp.where(row < COLS, states[d, 0:8], pltpu.roll(end, COLS, 0))
             after = jnp.maximum(d - 1, 0)
-            following = known(after, weights_g[1 - side])
+            end = ready + product
+            ready = known(after, weights_g[1 - side])
+            unpack_matrix(packed_b, after, 0, weights_b[1 - side])
             unpack_matrix(packed, jnp.maximum(d - 2, 0), 0, weights_g[side])
-            unpack_matrix(packed_b, after, 0, weights_b[1 - side])
-            end = ready + apply(spread(end, keep), weights_b[side])
-            ready = following
         return end, ready
 
     lax.fori_loop(0, GROUPS // 2, pair, (jnp.zeros((8, LANES), F32), known(last, even_g)))
 
 
-def solve(kernel, slots, *arrays):
+def solve(kernel, slots, rows, room, *arrays):
     return pl.pallas_call(
         kernel,
-        out_shape=jax.ShapeDtypeStruct((GROUPS, 8, LANES), F32),
+        out_shape=jax.ShapeDtypeStruct((GROUPS, rows, LANES), F32),
         in_specs=[whole()] * len(arrays),
         out_specs=whole(),
         scratch_shapes=[pltpu.VMEM((2 * LANES, 2 * LANES), BF16)] * slots,
         name=kernel.__name__,
-        **params(8, 7),
+        **params(room, 7),
     )(*arrays)
 
 
@@ -429,24 +483,24 @@
     delta = previous
     low, high = edges(delta)
     backward_maps = backward_products(upper_coupling, low)
-    forward_maps, chain = forward_products(lower_coupling, backward_maps)
-    backward_maps = exchange(backward_maps.reshape(GROUPS, ROWS, LANES))
-    forward_maps = forward_maps.reshape(GROUPS, FIRST, LANES)
     for sweep_index in range(SWEEPS):
         below = lax.ppermute(high, "surf", up)
         above = lax.ppermute(low, "surf", down)
         arrays = (
             rhs, delta, below, above, minus_jac, plus_jac, dissipation, inverse_diag, lower_coupling, upper_coupling
         )
+        room = ROOM if sweep_index == 0 else 8
         if sweep_index == 0:
-            source, forward_maps = local_source(*arrays, packed=forward_maps)
+            forward_maps, source, chain = forward_products(*arrays, backward_maps)
+            backward_maps = exchange(backward_maps)
+            across_maps = backward_products(upper_coupling, forward_maps, chain)
             forward_maps = vectors = exchange(forward_maps)
-            across_maps = exchange(backward_products(upper_coupling, source, chain).reshape(GROUPS, ROWS, LANES))
+            across_maps = exchange(across_maps)
         else:
             source, vectors = local_source(*arrays)
             vectors = exchange(vectors)
-        states = solve(forward_solve_kernel, 2, forward_maps, vectors)
-        incoming = exchange(solve(backward_solve_kernel, 4, across_maps, backward_maps, vectors, states))
+        states = solve(forward_solve_kernel, 2, 16, room, forward_maps, vectors)
+        incoming = exchange(solve(backward_solve_kernel, 4, 8, 8, across_maps, backward_maps, states))
         last = sweep_index == SWEEPS - 1
         delta, *sides = finish(
             last, incoming.reshape(GROUPS * 8, LANES), source, lower_coupling, upper_coupling

time: 174 us -> 168 us (0.966)
  local copies, waits for them, and re-layouts: 14 us -> 3.06 us
  Pallas kernels: 81.7 us -> 85.4 us
  waiting for transfers between devices: 11.1 us -> 14.1 us
    unnamed x54 -> x30, local copies, waits for them, and re-layouts: 14 us -> 3.06 us
    all_to_all x3, waiting for transfers between devices: 10.1 us -> 13.2 us  [exchange(): return lax.all_to_all(value, 'norm', 0, 0, tiled=True)]
    pallas_call x7 -> x6, Pallas kernels: 48.3 us -> 50.5 us  [the longest x4 27.2 us: solve(): pl.pallas_call(kernel, out_shape=jax.ShapeDtypeStruct((GROUPS, rows, LANE...]
    ppermute x2, starting transfers between devices: 4.01 us -> 5.94 us  [shards(): above = lax.ppermute(low, 'surf', down)]
  transfers between devices with their start and end apart: 7 -> 7, of which waited for: 2 -> 3; matrix products, arithmetic and copies ran while one was open for 0% -> 0% of each run, Pallas kernels for 31% -> 36%
where the time goes in v3:
time: 168 us; the launch traced here: 167 us
  Pallas kernels  85.4 us (51%)
  blocking collectives  35.4 us (21%)
  starting transfers between devices  29.1 us (17%)
  waiting for transfers between devices  14.1 us (8%)
  local copies, waits for them, and re-layouts  3.06 us (2%)
    all_to_all x3, blocking collectives, exchange(): return lax.all_to_all(value, 'norm', 0, 0, tiled=True)  35.4 us
    pallas_call x2, Pallas kernels, backward_products(): pl.pallas_call(across_kernel if across else backward_kernel, out_shape=ja...  31.8 us
    pallas_call x4, Pallas kernels, solve(): pl.pallas_call(kernel, out_shape=jax.ShapeDtypeStruct((GROUPS, rows, LANE...  27.2 us
    all_to_all x3, starting transfers between devices, exchange(): return lax.all_to_all(value, 'norm', 0, 0, tiled=True)  22.7 us
    pallas_call x1, Pallas kernels, forward_products(): pl.pallas_call(forward_kernel, out_shape=(jax.ShapeDtypeStruct((GROUPS, F...  20.5 us
    all_to_all x3, waiting for transfers between devices, exchange(): return lax.all_to_all(value, 'norm', 0, 0, tiled=True)  13.2 us
    ppermute x2, starting transfers between devices, shards(): above = lax.ppermute(low, 'surf', down)  5.94 us
  transfers between devices with their start and end apart: 7, of which 3 were waited for; matrix products, arithmetic and copies ran while one was open for 0% of the time, Pallas kernels for 36%

profile of v3, /device:TPU:1, one launch (start us, length us, event | category | flops | bytes accessed | tf_op | source)
XLA Modules:
  0.0 167.3 jit_solution(13640734110778142577)
XLA Ops:
  0.0 0.0 copy-start.9
  0.0 0.9 copy-done.9
  0.9 0.1 edges.1
  1.0 0.0 copy-start.10
  1.0 3.4 %collective-permute-start.1 = (f32[8,128]{1,0:T(8,128)S(1)}, f32[8,128]{1,0:T(8,128)S(1)}, u32[]{:S(2)}, u32[]{:S(2)}) collective-permute-start(f32[8,128]{1,0:T(8,128)S(1)} %get-tuple-element.16.after), channel_id=1, source_target_pairs={{32,0},{64,32},{96,64},{0,96},{33,1},{65,33},{97,65},{1,97},{34,2}... | collective-permute-start | bytes 12296 | tf_op jit(solution)/shard_map/ppermute | solution.py:488
  4.4 0.0 collective-permute-start
  4.4 0.0 copy-done.10
  4.4 15.6 %backward_products.1.after = f32[32,72,128]{2,1,0:T(8,128)} custom-call(bf16[4,48,48,128]{3,2,1,0:T(8,128)(2,1)} %upper.11, f32[8,128]{1,0:T(8,128)} %copy-done.10), custom_call_target="tpu_custom_call" | custom-call | flops 15000000512 | tf_op jit(solution)/shard_map/backward_products/pallas_call | solution.py:220
  20.0 9.1 %all-to-all-start.1 = ((f32[32,72,128]{2,1,0:T(8,128)}), f32[32,72,128]{2,1,0:T(8,128)S(1)}, u32[]{:S(2)}, u32[]{:S(2)}) async-start(f32[32,72,128]{2,1,0:T(8,128)} %backward_products.1.after), calls=%async_computation.1 | async-start | bytes 2359296 | tf_op jit(solution)/shard_map/all_to_all | solution.py:474
  29.1 0.0 collective-permute-done.1.above
  29.1 0.0 copy-start.13
  29.1 0.0 collective-permute-done.below
  29.1 0.6 copy-done.13
  29.7 0.0 copy-start.14
  29.7 0.6 copy-done.14
  30.2 20.5 %forward_products.1 = (f32[32,80,128]{2,1,0:T(8,128)}, f32[4,48,128]{2,1,0:T(8,128)}, f32[4,2304,128]{2,1,0:T(8,128)}) custom-call(f32[4,48,128]{2,1,0:T(8,128)} %rhs.3, f32[4,48,128]{2,1,0:T(8,128)} %delta.3, f32[8,128]{1,0:T(8,128)} %copy-done.14, f32[8,128]{1,0:T(8,128)} %copy-done.13, bf16[4,48,48,128]{3,2,1,0:T(8,128)(2,1)} %minus.3, ...), custom_call_target="tpu_custom_call" | custom-call | flops 16999999488 | tf_op jit(solution)/shard_map/forward_products/pallas_call | solution.py:167
  50.7 0.0 all-to-all-done.1.packed_b
  50.7 7.4 %all-to-all-start.2 = ((f32[32,80,128]{2,1,0:T(8,128)}), f32[32,80,128]{2,1,0:T(8,128)S(1)}, u32[]{:S(2)}, u32[]{:S(2)}) async-start(f32[32,80,128]{2,1,0:T(8,128)} %get-tuple-element.17.after), calls=%async_computation.2 | async-start | bytes 2621440 | tf_op jit(solution)/shard_map/all_to_all | solution.py:474
  58.1 16.2 %across_products.1 = f32[32,72,128]{2,1,0:T(8,128)} custom-call(bf16[4,48,48,128]{3,2,1,0:T(8,128)(2,1)} %upper.11, f32[32,80,128]{2,1,0:T(8,128)} %get-tuple-element.17.after, f32[4,2304,128]{2,1,0:T(8,128)} %get-tuple-element.18.chain), custom_call_target="tpu_custom_call" | custom-call | flops 15000000512 | tf_op jit(solution)/shard_map/across_products/pallas_call | solution.py:220
  74.4 2.9 %all-to-all-done.2.packed.vectors = f32[32,80,128]{2,1,0:T(8,128)S(1)} async-done(((f32[32,80,128]{2,1,0:T(8,128)}), f32[32,80,128]{2,1,0:T(8,128)S(1)}, u32[]{:S(2)}, u32[]{:S(2)}) %all-to-all-start.2) | async-done | bytes 1310752 | tf_op jit(solution)/shard_map/all_to_all | solution.py:474
  77.2 0.0 copy-start.5
  77.2 6.2 %all-to-all-start = ((f32[32,72,128]{2,1,0:T(8,128)}), f32[32,72,128]{2,1,0:T(8,128)}, u32[]{:S(2)}, u32[]{:S(2)}) async-start(f32[32,72,128]{2,1,0:T(8,128)} %across_products.1), calls=%async_computation | async-start | bytes 2359296 | tf_op jit(solution)/shard_map/all_to_all | solution.py:474
  83.4 0.0 copy-done.5
  83.5 7.5 %forward_solve_kernel.2.states = f32[32,16,128]{2,1,0:T(8,128)} custom-call(f32[32,80,128]{2,1,0:T(8,128)} %copy-done.5, f32[32,80,128]{2,1,0:T(8,128)} %copy-done.5), custom_call_target="tpu_custom_call" | custom-call | flops 7000000000 | tf_op jit(solution)/shard_map/forward_solve_kernel/pallas_call | solution.py:462
  91.0 0.0 copy-start.3
  91.0 10.3 %all-to-all-done.packed = f32[32,72,128]{2,1,0:T(8,128)} async-done(((f32[32,72,128]{2,1,0:T(8,128)}), f32[32,72,128]{2,1,0:T(8,128)}, u32[]{:S(2)}, u32[]{:S(2)}) %all-to-all-start) | async-done | bytes 1179680 | tf_op jit(solution)/shard_map/all_to_all | solution.py:474
  101.3 0.0 copy-start.12
  101.3 0.9 copy-done.12
  102.3 0.0 copy-start.4
  102.3 0.0 copy-start.11
  102.3 0.0 copy-start.2
  102.3 7.4 %backward_solve_kernel.2 = f32[32,8,128]{2,1,0:T(8,128)S(1)} custom-call(f32[32,72,128]{2,1,0:T(8,128)} %all-to-all-done.packed, f32[32,72,128]{2,1,0:T(8,128)S(1)} %all-to-all-done.1.packed_b, f32[32,16,128]{2,1,0:T(8,128)S(1)} %copy-done.12), custom_call_target="tpu_custom_call" | custom-call | flops 7000000000 | tf_op jit(solution)/shard_map/backward_solve_kernel/pallas_call | solution.py:462
  109.6 12.0 %all_to_all.30 = f32[32,8,128]{2,1,0:T(8,128)S(1)} all-to-all(f32[32,8,128]{2,1,0:T(8,128)S(1)} %backward_solve_kernel.2), channel_id=1, replica_groups=mesh['surf'=4,'norm'=32] {'norm'}, dimensions={0} | all-to-all | bytes 262144 | tf_op jit(solution)/shard_map/all_to_all | solution.py:474
  121.6 0.0 copy-done.3
  121.6 0.0 copy-done.4
  121.6 0.0 copy-done.11
  121.6 0.0 copy-start
  121.6 0.0 copy-start.1
  121.7 0.0 copy-start.7
  121.7 0.0 copy-start.8
  121.7 1.2 finish.2
  122.9 0.5 collective-permute-start.2
  123.5 2.6 %collective-permute-start.3 = (f32[8,128]{1,0:T(8,128)S(1)}, f32[8,128]{1,0:T(8,128)S(1)}, u32[]{:S(2)}, u32[]{:S(2)}) collective-permute-start(f32[8,128]{1,0:T(8,128)S(1)} %get-tuple-element.22), channel_id=1, source_target_pairs={{32,0},{64,32},{96,64},{0,96},{33,1},{65,33},{97,65},{1,97},{34,2}... | collective-permute-start | bytes 12296 | tf_op jit(solution)/shard_map/ppermute | solution.py:488
  126.0 0.9 collective-permute-done.2.below
  126.9 0.0 collective-permute-done.3.above
  126.9 0.0 copy-done.2
  126.9 0.0 copy-done
  126.9 0.0 copy-done.1
  127.0 0.0 copy-done.7
  127.0 0.0 copy-done.8
  127.0 0.0 copy-start.6
  127.0 2.8 %local_source.1 = (f32[4,48,128]{2,1,0:T(8,128)S(1)}, f32[32,8,128]{2,1,0:T(8,128)S(1)}) custom-call(f32[4,48,128]{2,1,0:T(8,128)S(1)} %copy-done.7, f32[4,48,128]{2,1,0:T(8,128)S(1)} %get-tuple-element.20.delta, f32[8,128]{1,0:T(8,128)S(1)} %collective-permute-done.2.below, f32[8,128]{1,0:T(8,128)S(1)} %collective-permute-done.3.above, ...), custom_call_target="tpu_custom_call" | custom-call | flops 3000000000 | tf_op jit(solution)/shard_map/local_source/pallas_call | solution.py:317
  129.8 12.1 %all_to_all.31.vectors = f32[32,8,128]{2,1,0:T(8,128)S(1)} all-to-all(f32[32,8,128]{2,1,0:T(8,128)S(1)} %get-tuple-element.23), channel_id=1, replica_groups=mesh['surf'=4,'norm'=32] {'norm'}, dimensions={0} | all-to-all | bytes 262144 | tf_op jit(solution)/shard_map/all_to_all | solution.py:474
  141.9 0.0 copy-done.6
  141.9 5.1 %forward_solve_kernel.3.states = f32[32,16,128]{2,1,0:T(8,128)S(1)} custom-call(f32[32,80,128]{2,1,0:T(8,128)S(1)} %copy-done.6, f32[32,8,128]{2,1,0:T(8,128)S(1)} %all_to_all.31.vectors), custom_call_target="tpu_custom_call" | custom-call | flops 7000000000 | tf_op jit(solution)/shard_map/forward_solve_kernel/pallas_call | solution.py:462
  147.0 7.2 %backward_solve_kernel.3 = f32[32,8,128]{2,1,0:T(8,128)S(1)} custom-call(f32[32,72,128]{2,1,0:T(8,128)} %all-to-all-done.packed, f32[32,72,128]{2,1,0:T(8,128)S(1)} %all-to-all-done.1.packed_b, f32[32,16,128]{2,1,0:T(8,128)S(1)} %forward_solve_kernel.3.states), custom_call_target="tpu_custom_call" | custom-call | flops 7000000000 | tf_op jit(solution)/shard_map/backward_solve_kernel/pallas_call | solution.py:462
  154.3 11.3 %all_to_all.32 = f32[32,8,128]{2,1,0:T(8,128)S(1)} all-to-all(f32[32,8,128]{2,1,0:T(8,128)S(1)} %backward_solve_kernel.3), channel_id=1, replica_groups=mesh['surf'=4,'norm'=32] {'norm'}, dimensions={0} | all-to-all | bytes 262144 | tf_op jit(solution)/shard_map/all_to_all | solution.py:474
  165.5 1.8 %finish.3 = f32[4,48,128]{2,1,0:T(8,128)} custom-call(f32[256,128]{1,0:T(8,128)S(1)} %bitcast.3, f32[4,48,128]{2,1,0:T(8,128)S(1)} %get-tuple-element.24.source, bf16[4,48,48,128]{3,2,1,0:T(8,128)(2,1)S(1)} %copy-done.4, bf16[4,48,48,128]{3,2,1,0:T(8,128)(2,1)S(1)} %copy-done.3), custom_call_target="tpu_custom_call" | custom-call | flops 1500000000 | tf_op jit(solution)/shard_map/finish/pallas_call | solution.py:350
Async XLA Ops:
  0.0 0.9 copy-start.9
  1.0 3.4 %copy-start.10 = (f32[8,128]{1,0:T(8,128)}, f32[8,128]{1,0:T(8,128)S(1)}, u32[]{:S(2)}) copy-start(f32[8,128]{1,0:T(8,128)S(1)} %get-tuple-element.16.after) | copy-start | bytes 12292
  1.0 28.1 %collective-permute-start.1 = (f32[8,128]{1,0:T(8,128)S(1)}, f32[8,128]{1,0:T(8,128)S(1)}, u32[]{:S(2)}, u32[]{:S(2)}) collective-permute-start(f32[8,128]{1,0:T(8,128)S(1)} %get-tuple-element.16.after), channel_id=1, source_target_pairs={{32,0},{64,32},{96,64},{0,96},{33,1},{65,33},{97,65},{1,97},{34,2}... | collective-permute-start | bytes 12296 | tf_op jit(solution)/shard_map/ppermute | solution.py:488
  4.4 24.7 %collective-permute-start = (f32[8,128]{1,0:T(8,128)S(1)}, f32[8,128]{1,0:T(8,128)S(1)}, u32[]{:S(2)}, u32[]{:S(2)}) collective-permute-start(f32[8,128]{1,0:T(8,128)S(1)} %get-tuple-element.15), channel_id=1, source_target_pairs={{0,32},{32,64},{64,96},{96,0},{1,33},{33,65},{65,97},{97,1},{2,34}... | collective-permute-start | bytes 12296 | tf_op jit(solution)/shard_map/ppermute | solution.py:487
  20.0 30.8 %all-to-all-start.1 = ((f32[32,72,128]{2,1,0:T(8,128)}), f32[32,72,128]{2,1,0:T(8,128)S(1)}, u32[]{:S(2)}, u32[]{:S(2)}) async-start(f32[32,72,128]{2,1,0:T(8,128)} %backward_products.1.after), calls=%async_computation.1 | async-start | bytes 2359296 | tf_op jit(solution)/shard_map/all_to_all | solution.py:474
  29.1 0.6 copy-start.13
  29.7 0.6 copy-start.14
  50.7 26.5 %all-to-all-start.2 = ((f32[32,80,128]{2,1,0:T(8,128)}), f32[32,80,128]{2,1,0:T(8,128)S(1)}, u32[]{:S(2)}, u32[]{:S(2)}) async-start(f32[32,80,128]{2,1,0:T(8,128)} %get-tuple-element.17.after), calls=%async_computation.2 | async-start | bytes 2621440 | tf_op jit(solution)/shard_map/all_to_all | solution.py:474
  77.2 6.2 %copy-start.5 = (f32[32,80,128]{2,1,0:T(8,128)}, f32[32,80,128]{2,1,0:T(8,128)S(1)}, u32[]{:S(2)}) copy-start(f32[32,80,128]{2,1,0:T(8,128)S(1)} %all-to-all-done.2.packed.vectors) | copy-start | bytes 3932164
  77.2 24.1 %all-to-all-start = ((f32[32,72,128]{2,1,0:T(8,128)}), f32[32,72,128]{2,1,0:T(8,128)}, u32[]{:S(2)}, u32[]{:S(2)}) async-start(f32[32,72,128]{2,1,0:T(8,128)} %across_products.1), calls=%async_computation | async-start | bytes 2359296 | tf_op jit(solution)/shard_map/all_to_all | solution.py:474
  91.0 30.6 %copy-start.3 = (bf16[4,48,48,128]{3,2,1,0:T(8,128)(2,1)S(1)}, bf16[4,48,48,128]{3,2,1,0:T(8,128)(2,1)}, u32[]{:S(2)}) copy-start(bf16[4,48,48,128]{3,2,1,0:T(8,128)(2,1)} %upper.11) | copy-start | bytes 7077892
  101.3 1.0 copy-start.12
  102.3 19.4 %copy-start.4 = (bf16[4,48,48,128]{3,2,1,0:T(8,128)(2,1)S(1)}, bf16[4,48,48,128]{3,2,1,0:T(8,128)(2,1)}, u32[]{:S(2)}) copy-start(bf16[4,48,48,128]{3,2,1,0:T(8,128)(2,1)} %lower.7) | copy-start | bytes 7077892
  102.3 19.4 %copy-start.11 = (f32[4,48,128]{2,1,0:T(8,128)S(1)}, f32[4,48,128]{2,1,0:T(8,128)}, u32[]{:S(2)}) copy-start(f32[4,48,128]{2,1,0:T(8,128)} %get-tuple-element.19.source) | copy-start | bytes 294916
  102.3 24.7 %copy-start.2 = (bf16[4,48,48,128]{3,2,1,0:T(8,128)(2,1)S(1)}, bf16[4,48,48,128]{3,2,1,0:T(8,128)(2,1)}, u32[]{:S(2)}) copy-start(bf16[4,48,48,128]{3,2,1,0:T(8,128)(2,1)} %inverse.3) | copy-start | bytes 7077892
  121.6 5.3 %copy-start = (bf16[4,48,48,128]{3,2,1,0:T(8,128)(2,1)S(1)}, bf16[4,48,48,128]{3,2,1,0:T(8,128)(2,1)}, u32[]{:S(2)}) copy-start(bf16[4,48,48,128]{3,2,1,0:T(8,128)(2,1)} %minus.3) | copy-start | bytes 7077892
  121.6 5.3 %copy-start.1 = (bf16[4,48,48,128]{3,2,1,0:T(8,128)(2,1)S(1)}, bf16[4,48,48,128]{3,2,1,0:T(8,128)(2,1)}, u32[]{:S(2)}) copy-start(bf16[4,48,48,128]{3,2,1,0:T(8,128)(2,1)} %plus.3) | copy-start | bytes 7077892
  121.7 5.3 %copy-start.7 = (f32[4,48,128]{2,1,0:T(8,128)S(1)}, f32[4,48,128]{2,1,0:T(8,128)}, u32[]{:S(2)}) copy-start(f32[4,48,128]{2,1,0:T(8,128)} %rhs.3) | copy-start | bytes 294916
  121.7 5.3 %copy-start.8 = (f32[4,48,128]{2,1,0:T(8,128)S(1)}, f32[4,48,128]{2,1,0:T(8,128)}, u32[]{:S(2)}) copy-start(f32[4,48,128]{2,1,0:T(8,128)} %dissipation.3) | copy-start | bytes 294916
  122.9 4.0 %collective-permute-start.2 = (f32[8,128]{1,0:T(8,128)S(1)}, f32[8,128]{1,0:T(8,128)S(1)}, u32[]{:S(2)}, u32[]{:S(2)}) collective-permute-start(f32[8,128]{1,0:T(8,128)S(1)} %get-tuple-element.21), channel_id=1, source_target_pairs={{0,32},{32,64},{64,96},{96,0},{1,33},{33,65},{65,97},{97,1},{2,34}... | collective-permute-start | bytes 12296 | tf_op jit(solution)/shard_map/ppermute | solution.py:487
  123.5 3.5 %collective-permute-start.3 = (f32[8,128]{1,0:T(8,128)S(1)}, f32[8,128]{1,0:T(8,128)S(1)}, u32[]{:S(2)}, u32[]{:S(2)}) collective-permute-start(f32[8,128]{1,0:T(8,128)S(1)} %get-tuple-element.22), channel_id=1, source_target_pairs={{32,0},{64,32},{96,64},{0,96},{33,1},{65,33},{97,65},{1,97},{34,2}... | collective-permute-start | bytes 12296 | tf_op jit(solution)/shard_map/ppermute | solution.py:488
  127.0 14.9 %copy-start.6 = (f32[32,80,128]{2,1,0:T(8,128)S(1)}, f32[32,80,128]{2,1,0:T(8,128)}, u32[]{:S(2)}) copy-start(f32[32,80,128]{2,1,0:T(8,128)} %copy-done.5) | copy-start | bytes 3932164

commit v4 on v3

--- a/solution.py
+++ b/solution.py
@@ -181,7 +181,7 @@
             pltpu.VMEM((GROUPS, 8, LANES), F32),
         ],
         name="forward_products",
-        **params(ROOM - 5, 17),
+        **params(ROOM - 8, 17),
     )(*arrays)
 
 
@@ -458,6 +458,32 @@
     lax.fori_loop(0, GROUPS // 2, pair, (jnp.zeros((8, LANES), F32), known(last, even_g)))
 
 
+def solve_kernel(packed, vectors, across, packed_b, out, *rest):
+    *weights, states, held, sem = rest
+    copy = pltpu.make_async_copy(across, held, sem)
+    copy.start()
+    forward_solve_kernel(packed, vectors, states, *weights[:2])
+    copy.wait()
+    backward_solve_kernel(held, packed_b, states, out, *weights[2:])
+
+
+def solve_both(*arrays):
+    return pl.pallas_call(
+        solve_kernel,
+        out_shape=jax.ShapeDtypeStruct((GROUPS, 8, LANES), F32),
+        in_specs=[whole(), whole(), in_hbm(), whole()],
+        out_specs=whole(),
+        scratch_shapes=[pltpu.VMEM((2 * LANES, 2 * LANES), BF16)] * 6
+        + [
+            pltpu.VMEM((GROUPS, 16, LANES), F32),
+            pltpu.VMEM((GROUPS, ROWS, LANES), F32),
+            pltpu.SemaphoreType.DMA,
+        ],
+        name="solve_both",
+        **params(12, 12),
+    )(*arrays)
+
+
 def solve(kernel, slots, rows, room, *arrays):
     return pl.pallas_call(
         kernel,
@@ -489,7 +515,6 @@
         arrays = (
             rhs, delta, below, above, minus_jac, plus_jac, dissipation, inverse_diag, lower_coupling, upper_coupling
         )
-        room = ROOM if sweep_index == 0 else 8
         if sweep_index == 0:
             forward_maps, source, chain = forward_products(*arrays, backward_maps)
             backward_maps = exchange(backward_maps)
@@ -499,8 +524,12 @@
         else:
             source, vectors = local_source(*arrays)
             vectors = exchange(vectors)
-        states = solve(forward_solve_kernel, 2, 16, room, forward_maps, vectors)
-        incoming = exchange(solve(backward_solve_kernel, 4, 8, 8, across_maps, backward_maps, states))
+        if sweep_index == 0:
+            states = solve(forward_solve_kernel, 2, 16, ROOM, forward_maps, vectors)
+            incoming = solve(backward_solve_kernel, 4, 8, 8, across_maps, backward_maps, states)
+        else:
+            incoming = solve_both(forward_maps, vectors, across_maps, backward_maps)
+        incoming = exchange(incoming)
         last = sweep_index == SWEEPS - 1
         delta, *sides = finish(
             last, incoming.reshape(GROUPS * 8, LANES), source, lower_coupling, upper_coupling

time: 168 us -> 165 us (0.982)
  Pallas kernels: 85.4 us -> 82.6 us
    pallas_call x4 -> x2, Pallas kernels: 27.2 us -> 14.9 us  [solve(): pl.pallas_call(kernel, out_shape=jax.ShapeDtypeStruct((GROUPS, rows, LANE...]
    pallas_call x0 -> x1, Pallas kernels: none -> 11.1 us  [solve_both(): pl.pallas_call(solve_kernel, out_shape=jax.ShapeDtypeStruct((GROUPS, 8, L...]
  transfers between devices with their start and end apart: 7 -> 7, of which waited for: 3 -> 3; matrix products, arithmetic and copies ran while one was open for 0% -> 0% of each run, Pallas kernels for 36% -> 35%
where the time goes in v4:
time: 165 us; the launch traced here: 164 us
  Pallas kernels  82.6 us (50%)
  blocking collectives  35.4 us (21%)
  starting transfers between devices  29.3 us (18%)
  waiting for transfers between devices  14.1 us (9%)
  local copies, waits for them, and re-layouts  2.55 us (2%)
    all_to_all x3, blocking collectives, exchange(): return lax.all_to_all(value, 'norm', 0, 0, tiled=True)  35.4 us
    pallas_call x2, Pallas kernels, backward_products(): pl.pallas_call(across_kernel if across else backward_kernel, out_shape=ja...  31.8 us
    all_to_all x3, starting transfers between devices, exchange(): return lax.all_to_all(value, 'norm', 0, 0, tiled=True)  22.8 us
    pallas_call x1, Pallas kernels, forward_products(): pl.pallas_call(forward_kernel, out_shape=(jax.ShapeDtypeStruct((GROUPS, F...  18.9 us
    pallas_call x2, Pallas kernels, solve(): pl.pallas_call(kernel, out_shape=jax.ShapeDtypeStruct((GROUPS, rows, LANE...  14.9 us
    all_to_all x3, waiting for transfers between devices, exchange(): return lax.all_to_all(value, 'norm', 0, 0, tiled=True)  13.2 us
    pallas_call x1, Pallas kernels, solve_both(): pl.pallas_call(solve_kernel, out_shape=jax.ShapeDtypeStruct((GROUPS, 8, L...  11.1 us
    ppermute x2, starting transfers between devices, shards(): above = lax.ppermute(low, 'surf', down)  5.94 us
  transfers between devices with their start and end apart: 7, of which 3 were waited for; matrix products, arithmetic and copies ran while one was open for 0% of the time, Pallas kernels for 35%

profile of v4, /device:TPU:1, one launch (start us, length us, event | category | flops | bytes accessed | tf_op | source)
XLA Modules:
  0.0 164.2 jit_solution(17421805097520858418)
XLA Ops:
  0.0 0.0 copy-start.12
  0.0 0.9 copy-done.12
  0.9 0.1 edges.1
  1.0 0.0 copy-start.14
  1.0 3.4 %collective-permute-start.1 = (f32[8,128]{1,0:T(8,128)S(1)}, f32[8,128]{1,0:T(8,128)S(1)}, u32[]{:S(2)}, u32[]{:S(2)}) collective-permute-start(f32[8,128]{1,0:T(8,128)S(1)} %get-tuple-element.16.after), channel_id=1, source_target_pairs={{32,0},{64,32},{96,64},{0,96},{33,1},{65,33},{97,65},{1,97},{34,2}... | collective-permute-start | bytes 12296 | tf_op jit(solution)/shard_map/ppermute | solution.py:514
  4.4 0.0 collective-permute-start
  4.4 0.0 copy-done.14
  4.4 15.6 %backward_products.1.after = f32[32,72,128]{2,1,0:T(8,128)} custom-call(bf16[4,48,48,128]{3,2,1,0:T(8,128)(2,1)} %upper.11, f32[8,128]{1,0:T(8,128)} %copy-done.14), custom_call_target="tpu_custom_call" | custom-call | flops 15000000512 | tf_op jit(solution)/shard_map/backward_products/pallas_call | solution.py:220
  20.0 0.0 copy-start.7
  20.0 0.0 copy-start.8
  20.0 0.0 copy-start.10
  20.0 0.0 copy-start.13
  20.0 9.2 %all-to-all-start.2 = ((f32[32,72,128]{2,1,0:T(8,128)}), f32[32,72,128]{2,1,0:T(8,128)S(1)}, u32[]{:S(2)}, u32[]{:S(2)}) async-start(f32[32,72,128]{2,1,0:T(8,128)} %backward_products.1.after), calls=%async_computation.2 | async-start | bytes 2359296 | tf_op jit(solution)/shard_map/all_to_all | solution.py:500
  29.2 0.0 collective-permute-done.1.above
  29.2 0.0 collective-permute-done.below
  29.3 0.0 copy-done.7
  29.3 0.0 copy-done.8
  29.3 0.0 copy-done.10
  29.3 0.0 copy-done.13
  29.3 18.9 %forward_products.1 = (f32[32,80,128]{2,1,0:T(8,128)}, f32[4,48,128]{2,1,0:T(8,128)S(1)}, f32[4,2304,128]{2,1,0:T(8,128)}) custom-call(f32[4,48,128]{2,1,0:T(8,128)S(1)} %copy-done.8, f32[4,48,128]{2,1,0:T(8,128)S(1)} %copy-done.13, f32[8,128]{1,0:T(8,128)S(1)} %collective-permute-done.below, f32[8,128]{1,0:T(8,128)S(1)} %collective-permute-done.1.above, ...), custom_call_target="tpu_custom_call" | custom-call | flops 16999999488 | tf_op jit(solution)/shard_map/forward_products/pallas_call | solution.py:167
  48.2 0.0 copy-start.15
  48.2 0.6 copy-done.15
  48.8 0.0 all-to-all-done.2.packed_b
  48.8 7.4 %all-to-all-start = ((f32[32,80,128]{2,1,0:T(8,128)}), f32[32,80,128]{2,1,0:T(8,128)S(1)}, u32[]{:S(2)}, u32[]{:S(2)}) async-start(f32[32,80,128]{2,1,0:T(8,128)} %get-tuple-element.17.after), calls=%async_computation | async-start | bytes 2621440 | tf_op jit(solution)/shard_map/all_to_all | solution.py:500
  56.2 16.2 %across_products.1 = f32[32,72,128]{2,1,0:T(8,128)} custom-call(bf16[4,48,48,128]{3,2,1,0:T(8,128)(2,1)} %upper.11, f32[32,80,128]{2,1,0:T(8,128)} %get-tuple-element.17.after, f32[4,2304,128]{2,1,0:T(8,128)} %get-tuple-element.18.chain), custom_call_target="tpu_custom_call" | custom-call | flops 15000000512 | tf_op jit(solution)/shard_map/across_products/pallas_call | solution.py:220
  72.4 2.9 %all-to-all-done.packed.vectors = f32[32,80,128]{2,1,0:T(8,128)S(1)} async-done(((f32[32,80,128]{2,1,0:T(8,128)}), f32[32,80,128]{2,1,0:T(8,128)S(1)}, u32[]{:S(2)}, u32[]{:S(2)}) %all-to-all-start) | async-done | bytes 1310752 | tf_op jit(solution)/shard_map/all_to_all | solution.py:500
  75.3 0.0 copy-start.5
  75.3 6.2 %all-to-all-start.1 = ((f32[32,72,128]{2,1,0:T(8,128)}), f32[32,72,128]{2,1,0:T(8,128)}, u32[]{:S(2)}, u32[]{:S(2)}) async-start(f32[32,72,128]{2,1,0:T(8,128)} %across_products.1), calls=%async_computation.1 | async-start | bytes 2359296 | tf_op jit(solution)/shard_map/all_to_all | solution.py:500
  81.5 0.0 copy-done.5
  81.5 7.6 %forward_solve_kernel.1.states = f32[32,16,128]{2,1,0:T(8,128)} custom-call(f32[32,80,128]{2,1,0:T(8,128)} %copy-done.5, f32[32,80,128]{2,1,0:T(8,128)} %copy-done.5), custom_call_target="tpu_custom_call" | custom-call | flops 7000000000 | tf_op jit(solution)/shard_map/forward_solve_kernel/pallas_call | solution.py:488
  89.1 0.0 copy-start.3
  89.1 10.3 %all-to-all-done.1.packed.across = f32[32,72,128]{2,1,0:T(8,128)} async-done(((f32[32,72,128]{2,1,0:T(8,128)}), f32[32,72,128]{2,1,0:T(8,128)}, u32[]{:S(2)}, u32[]{:S(2)}) %all-to-all-start.1) | async-done | bytes 1179680 | tf_op jit(solution)/shard_map/all_to_all | solution.py:500
  99.4 0.0 copy-start.17
  99.4 0.9 copy-done.17
  100.3 0.0 copy-start.4
  100.3 0.0 copy-start.16
  100.3 0.0 copy-start.2
  100.3 7.4 %backward_solve_kernel.1 = f32[32,8,128]{2,1,0:T(8,128)S(1)} custom-call(f32[32,72,128]{2,1,0:T(8,128)} %all-to-all-done.1.packed.across, f32[32,72,128]{2,1,0:T(8,128)S(1)} %all-to-all-done.2.packed_b, f32[32,16,128]{2,1,0:T(8,128)S(1)} %copy-done.17), custom_call_target="tpu_custom_call" | custom-call | flops 7000000000 | tf_op jit(solution)/shard_map/backward_solve_kernel/pallas_call | solution.py:488
  107.7 12.0 %all_to_all.30 = f32[32,8,128]{2,1,0:T(8,128)S(1)} all-to-all(f32[32,8,128]{2,1,0:T(8,128)S(1)} %backward_solve_kernel.1), channel_id=1, replica_groups=mesh['surf'=4,'norm'=32] {'norm'}, dimensions={0} | all-to-all | bytes 262144 | tf_op jit(solution)/shard_map/all_to_all | solution.py:500
  119.7 0.0 copy-done.3
  119.7 0.0 copy-done.4
  119.7 0.0 copy-done.16
  119.7 0.0 copy-start
  119.7 0.0 copy-start.1
  119.7 0.0 copy-start.9
  119.7 0.0 copy-start.11
  119.7 1.2 finish.2
  121.0 0.5 collective-permute-start.2
  121.5 2.6 %collective-permute-start.3 = (f32[8,128]{1,0:T(8,128)S(1)}, f32[8,128]{1,0:T(8,128)S(1)}, u32[]{:S(2)}, u32[]{:S(2)}) collective-permute-start(f32[8,128]{1,0:T(8,128)S(1)} %get-tuple-element.22), channel_id=1, source_target_pairs={{32,0},{64,32},{96,64},{0,96},{33,1},{65,33},{97,65},{1,97},{34,2}... | collective-permute-start | bytes 12296 | tf_op jit(solution)/shard_map/ppermute | solution.py:514
  124.1 0.9 collective-permute-done.2.below
  125.0 0.0 collective-permute-done.3.above
  125.0 0.0 copy-done.2
  125.0 0.0 copy-done
  125.0 0.0 copy-done.1
  125.0 0.0 copy-done.9
  125.0 0.0 copy-done.11
  125.0 0.0 copy-start.6
  125.1 2.8 %local_source.1 = (f32[4,48,128]{2,1,0:T(8,128)S(1)}, f32[32,8,128]{2,1,0:T(8,128)S(1)}) custom-call(f32[4,48,128]{2,1,0:T(8,128)S(1)} %copy-done.9, f32[4,48,128]{2,1,0:T(8,128)S(1)} %get-tuple-element.20.delta, f32[8,128]{1,0:T(8,128)S(1)} %collective-permute-done.2.below, f32[8,128]{1,0:T(8,128)S(1)} %collective-permute-done.3.above, ...), custom_call_target="tpu_custom_call" | custom-call | flops 3000000000 | tf_op jit(solution)/shard_map/local_source/pallas_call | solution.py:317
  127.8 12.1 %all_to_all.31.vectors = f32[32,8,128]{2,1,0:T(8,128)S(1)} all-to-all(f32[32,8,128]{2,1,0:T(8,128)S(1)} %get-tuple-element.23), channel_id=1, replica_groups=mesh['surf'=4,'norm'=32] {'norm'}, dimensions={0} | all-to-all | bytes 262144 | tf_op jit(solution)/shard_map/all_to_all | solution.py:500
  140.0 0.0 copy-done.6
  140.0 11.1 %solve_both.1 = f32[32,8,128]{2,1,0:T(8,128)S(1)} custom-call(f32[32,80,128]{2,1,0:T(8,128)S(1)} %copy-done.6, f32[32,8,128]{2,1,0:T(8,128)S(1)} %all_to_all.31.vectors, f32[32,72,128]{2,1,0:T(8,128)} %all-to-all-done.1.packed.across, f32[32,72,128]{2,1,0:T(8,128)S(1)} %all-to-all-done.2.packed_b), custom_call_target="tpu_custom_call" | custom-call | flops 12000000000 | tf_op jit(solution)/shard_map/solve_both/pallas_call | solution.py:471
  151.1 11.3 %all_to_all.32 = f32[32,8,128]{2,1,0:T(8,128)S(1)} all-to-all(f32[32,8,128]{2,1,0:T(8,128)S(1)} %solve_both.1), channel_id=1, replica_groups=mesh['surf'=4,'norm'=32] {'norm'}, dimensions={0} | all-to-all | bytes 262144 | tf_op jit(solution)/shard_map/all_to_all | solution.py:500
  162.3 1.8 %finish.3 = f32[4,48,128]{2,1,0:T(8,128)} custom-call(f32[256,128]{1,0:T(8,128)S(1)} %bitcast.3, f32[4,48,128]{2,1,0:T(8,128)S(1)} %get-tuple-element.24.source, bf16[4,48,48,128]{3,2,1,0:T(8,128)(2,1)S(1)} %copy-done.3, bf16[4,48,48,128]{3,2,1,0:T(8,128)(2,1)S(1)} %copy-done.4), custom_call_target="tpu_custom_call" | custom-call | flops 1500000000 | tf_op jit(solution)/shard_map/finish/pallas_call | solution.py:350
Async XLA Ops:
  0.0 0.9 copy-start.12
  1.0 3.4 %copy-start.14 = (f32[8,128]{1,0:T(8,128)}, f32[8,128]{1,0:T(8,128)S(1)}, u32[]{:S(2)}) copy-start(f32[8,128]{1,0:T(8,128)S(1)} %get-tuple-element.16.after) | copy-start | bytes 12292
  1.0 28.2 %collective-permute-start.1 = (f32[8,128]{1,0:T(8,128)S(1)}, f32[8,128]{1,0:T(8,128)S(1)}, u32[]{:S(2)}, u32[]{:S(2)}) collective-permute-start(f32[8,128]{1,0:T(8,128)S(1)} %get-tuple-element.16.after), channel_id=1, source_target_pairs={{32,0},{64,32},{96,64},{0,96},{33,1},{65,33},{97,65},{1,97},{34,2}... | collective-permute-start | bytes 12296 | tf_op jit(solution)/shard_map/ppermute | solution.py:514
  4.4 24.9 %collective-permute-start = (f32[8,128]{1,0:T(8,128)S(1)}, f32[8,128]{1,0:T(8,128)S(1)}, u32[]{:S(2)}, u32[]{:S(2)}) collective-permute-start(f32[8,128]{1,0:T(8,128)S(1)} %get-tuple-element.15), channel_id=1, source_target_pairs={{0,32},{32,64},{64,96},{96,0},{1,33},{33,65},{65,97},{97,1},{2,34}... | collective-permute-start | bytes 12296 | tf_op jit(solution)/shard_map/ppermute | solution.py:513
  20.0 9.3 %copy-start.7 = (f32[32,72,128]{2,1,0:T(8,128)S(1)}, f32[32,72,128]{2,1,0:T(8,128)}, u32[]{:S(2)}) copy-start(f32[32,72,128]{2,1,0:T(8,128)} %backward_products.1.after) | copy-start | bytes 3538948
  20.0 9.3 %copy-start.8 = (f32[4,48,128]{2,1,0:T(8,128)S(1)}, f32[4,48,128]{2,1,0:T(8,128)}, u32[]{:S(2)}) copy-start(f32[4,48,128]{2,1,0:T(8,128)} %rhs.3) | copy-start | bytes 294916
  20.0 9.3 %copy-start.10 = (f32[4,48,128]{2,1,0:T(8,128)S(1)}, f32[4,48,128]{2,1,0:T(8,128)}, u32[]{:S(2)}) copy-start(f32[4,48,128]{2,1,0:T(8,128)} %dissipation.3) | copy-start | bytes 294916
  20.0 9.3 %copy-start.13 = (f32[4,48,128]{2,1,0:T(8,128)S(1)}, f32[4,48,128]{2,1,0:T(8,128)}, u32[]{:S(2)}) copy-start(f32[4,48,128]{2,1,0:T(8,128)} %delta.3) | copy-start | bytes 294916
  20.0 28.8 %all-to-all-start.2 = ((f32[32,72,128]{2,1,0:T(8,128)}), f32[32,72,128]{2,1,0:T(8,128)S(1)}, u32[]{:S(2)}, u32[]{:S(2)}) async-start(f32[32,72,128]{2,1,0:T(8,128)} %backward_products.1.after), calls=%async_computation.2 | async-start | bytes 2359296 | tf_op jit(solution)/shard_map/all_to_all | solution.py:500
  48.2 0.6 copy-start.15
  48.8 26.5 %all-to-all-start = ((f32[32,80,128]{2,1,0:T(8,128)}), f32[32,80,128]{2,1,0:T(8,128)S(1)}, u32[]{:S(2)}, u32[]{:S(2)}) async-start(f32[32,80,128]{2,1,0:T(8,128)} %get-tuple-element.17.after), calls=%async_computation | async-start | bytes 2621440 | tf_op jit(solution)/shard_map/all_to_all | solution.py:500
  75.3 6.2 %copy-start.5 = (f32[32,80,128]{2,1,0:T(8,128)}, f32[32,80,128]{2,1,0:T(8,128)S(1)}, u32[]{:S(2)}) copy-start(f32[32,80,128]{2,1,0:T(8,128)S(1)} %all-to-all-done.packed.vectors) | copy-start | bytes 3932164
  75.3 24.1 %all-to-all-start.1 = ((f32[32,72,128]{2,1,0:T(8,128)}), f32[32,72,128]{2,1,0:T(8,128)}, u32[]{:S(2)}, u32[]{:S(2)}) async-start(f32[32,72,128]{2,1,0:T(8,128)} %across_products.1), calls=%async_computation.1 | async-start | bytes 2359296 | tf_op jit(solution)/shard_map/all_to_all | solution.py:500
  89.1 30.6 %copy-start.3 = (bf16[4,48,48,128]{3,2,1,0:T(8,128)(2,1)S(1)}, bf16[4,48,48,128]{3,2,1,0:T(8,128)(2,1)}, u32[]{:S(2)}) copy-start(bf16[4,48,48,128]{3,2,1,0:T(8,128)(2,1)} %lower.7) | copy-start | bytes 7077892
  99.4 1.0 copy-start.17
  100.3 19.4 %copy-start.4 = (bf16[4,48,48,128]{3,2,1,0:T(8,128)(2,1)S(1)}, bf16[4,48,48,128]{3,2,1,0:T(8,128)(2,1)}, u32[]{:S(2)}) copy-start(bf16[4,48,48,128]{3,2,1,0:T(8,128)(2,1)} %upper.11) | copy-start | bytes 7077892
  100.3 19.4 %copy-start.16 = (f32[4,48,128]{2,1,0:T(8,128)S(1)}, f32[4,48,128]{2,1,0:T(8,128)}, u32[]{:S(2)}) copy-start(f32[4,48,128]{2,1,0:T(8,128)} %copy-done.15) | copy-start | bytes 294916
  100.3 24.7 %copy-start.2 = (bf16[4,48,48,128]{3,2,1,0:T(8,128)(2,1)S(1)}, bf16[4,48,48,128]{3,2,1,0:T(8,128)(2,1)}, u32[]{:S(2)}) copy-start(bf16[4,48,48,128]{3,2,1,0:T(8,128)(2,1)} %inverse.3) | copy-start | bytes 7077892
  119.7 5.3 %copy-start = (bf16[4,48,48,128]{3,2,1,0:T(8,128)(2,1)S(1)}, bf16[4,48,48,128]{3,2,1,0:T(8,128)(2,1)}, u32[]{:S(2)}) copy-start(bf16[4,48,48,128]{3,2,1,0:T(8,128)(2,1)} %minus.3) | copy-start | bytes 7077892
  119.7 5.3 %copy-start.1 = (bf16[4,48,48,128]{3,2,1,0:T(8,128)(2,1)S(1)}, bf16[4,48,48,128]{3,2,1,0:T(8,128)(2,1)}, u32[]{:S(2)}) copy-start(bf16[4,48,48,128]{3,2,1,0:T(8,128)(2,1)} %plus.3) | copy-start | bytes 7077892
  119.7 5.3 %copy-start.9 = (f32[4,48,128]{2,1,0:T(8,128)S(1)}, f32[4,48,128]{2,1,0:T(8,128)}, u32[]{:S(2)}) copy-start(f32[4,48,128]{2,1,0:T(8,128)} %rhs.3) | copy-start | bytes 294916
  119.7 5.3 %copy-start.11 = (f32[4,48,128]{2,1,0:T(8,128)S(1)}, f32[4,48,128]{2,1,0:T(8,128)}, u32[]{:S(2)}) copy-start(f32[4,48,128]{2,1,0:T(8,128)} %dissipation.3) | copy-start | bytes 294916
  121.0 4.0 %collective-permute-start.2 = (f32[8,128]{1,0:T(8,128)S(1)}, f32[8,128]{1,0:T(8,128)S(1)}, u32[]{:S(2)}, u32[]{:S(2)}) collective-permute-start(f32[8,128]{1,0:T(8,128)S(1)} %get-tuple-element.21), channel_id=1, source_target_pairs={{0,32},{32,64},{64,96},{96,0},{1,33},{33,65},{65,97},{97,1},{2,34}... | collective-permute-start | bytes 12296 | tf_op jit(solution)/shard_map/ppermute | solution.py:513
  121.5 3.5 %collective-permute-start.3 = (f32[8,128]{1,0:T(8,128)S(1)}, f32[8,128]{1,0:T(8,128)S(1)}, u32[]{:S(2)}, u32[]{:S(2)}) collective-permute-start(f32[8,128]{1,0:T(8,128)S(1)} %get-tuple-element.22), channel_id=1, source_target_pairs={{32,0},{64,32},{96,64},{0,96},{33,1},{65,33},{97,65},{1,97},{34,2}... | collective-permute-start | bytes 12296 | tf_op jit(solution)/shard_map/ppermute | solution.py:514
  125.0 14.9 %copy-start.6 = (f32[32,80,128]{2,1,0:T(8,128)S(1)}, f32[32,80,128]{2,1,0:T(8,128)}, u32[]{:S(2)}) copy-start(f32[32,80,128]{2,1,0:T(8,128)} %copy-done.5) | copy-start | bytes 3932164

commit v5 on v4

--- a/solution.py
+++ b/solution.py
@@ -423,7 +423,7 @@
             state = vector + product
         return state
 
-    lax.fori_loop(0, GROUPS // 2, pair, jnp.zeros((8, LANES), F32))
+    lax.fori_loop(0, GROUPS // 2, pair, jnp.zeros((8, LANES), F32), unroll=4)
 
 
 def backward_solve_kernel(packed, packed_b, states, out, even_g, odd_g, even_b, odd_b):
@@ -455,7 +455,7 @@
             unpack_matrix(packed, jnp.maximum(d - 2, 0), 0, weights_g[side])
         return end, ready
 
-    lax.fori_loop(0, GROUPS // 2, pair, (jnp.zeros((8, LANES), F32), known(last, even_g)))
+    lax.fori_loop(0, GROUPS // 2, pair, (jnp.zeros((8, LANES), F32), known(last, even_g)), unroll=4)
 
 
 def solve_kernel(packed, vectors, across, packed_b, out, *rest):

time: 165 us -> 163 us (0.988)
  Pallas kernels: 82.6 us -> 79.7 us
  transfers between devices with their start and end apart: 7 -> 7, of which waited for: 3 -> 3; matrix products, arithmetic and copies ran while one was open for 0% -> 0% of each run, Pallas kernels for 35% -> 36%
where the time goes in v5:
time: 163 us; the launch traced here: 162 us
  Pallas kernels  79.7 us (49%)
  blocking collectives  35.4 us (22%)
  starting transfers between devices  29.3 us (18%)
  waiting for transfers between devices  14.8 us (9%)
  local copies, waits for them, and re-layouts  2.55 us (2%)
    all_to_all x3, blocking collectives, exchange(): return lax.all_to_all(value, 'norm', 0, 0, tiled=True)  35.4 us
    pallas_call x2, Pallas kernels, backward_products(): pl.pallas_call(across_kernel if across else backward_kernel, out_shape=ja...  31.8 us
    all_to_all x3, starting transfers between devices, exchange(): return lax.all_to_all(value, 'norm', 0, 0, tiled=True)  22.8 us
    pallas_call x1, Pallas kernels, forward_products(): pl.pallas_call(forward_kernel, out_shape=(jax.ShapeDtypeStruct((GROUPS, F...  18.9 us
    all_to_all x3, waiting for transfers between devices, exchange(): return lax.all_to_all(value, 'norm', 0, 0, tiled=True)  13.8 us
    pallas_call x2, Pallas kernels, solve(): pl.pallas_call(kernel, out_shape=jax.ShapeDtypeStruct((GROUPS, rows, LANE...  13.5 us
    pallas_call x1, Pallas kernels, solve_both(): pl.pallas_call(solve_kernel, out_shape=jax.ShapeDtypeStruct((GROUPS, 8, L...  9.7 us
    ppermute x2, starting transfers between devices, shards(): above = lax.ppermute(low, 'surf', down)  5.94 us
  transfers between devices with their start and end apart: 7, of which 3 were waited for; matrix products, arithmetic and copies ran while one was open for 0% of the time, Pallas kernels for 36%

profile of v5, /device:TPU:1, one launch (start us, length us, event | category | flops | bytes accessed | tf_op | source)
XLA Modules:
  0.0 162.0 jit_solution(5508668290841690357)
XLA Ops:
  0.0 0.0 copy-start.12
  0.0 0.9 copy-done.12
  0.9 0.1 edges.1
  1.0 0.0 copy-start.14
  1.0 3.4 %collective-permute-start.1 = (f32[8,128]{1,0:T(8,128)S(1)}, f32[8,128]{1,0:T(8,128)S(1)}, u32[]{:S(2)}, u32[]{:S(2)}) collective-permute-start(f32[8,128]{1,0:T(8,128)S(1)} %get-tuple-element.16.after), channel_id=1, source_target_pairs={{32,0},{64,32},{96,64},{0,96},{33,1},{65,33},{97,65},{1,97},{34,2}... | collective-permute-start | bytes 12296 | tf_op jit(solution)/shard_map/ppermute | solution.py:514
  4.4 0.0 collective-permute-start
  4.4 0.0 copy-done.14
  4.4 15.6 %backward_products.1.after = f32[32,72,128]{2,1,0:T(8,128)} custom-call(bf16[4,48,48,128]{3,2,1,0:T(8,128)(2,1)} %upper.11, f32[8,128]{1,0:T(8,128)} %copy-done.14), custom_call_target="tpu_custom_call" | custom-call | flops 15000000512 | tf_op jit(solution)/shard_map/backward_products/pallas_call | solution.py:220
  20.0 0.0 copy-start.7
  20.0 0.0 copy-start.8
  20.0 0.0 copy-start.10
  20.0 0.0 copy-start.13
  20.0 9.2 %all-to-all-start.2 = ((f32[32,72,128]{2,1,0:T(8,128)}), f32[32,72,128]{2,1,0:T(8,128)S(1)}, u32[]{:S(2)}, u32[]{:S(2)}) async-start(f32[32,72,128]{2,1,0:T(8,128)} %backward_products.1.after), calls=%async_computation.2 | async-start | bytes 2359296 | tf_op jit(solution)/shard_map/all_to_all | solution.py:500
  29.2 0.0 collective-permute-done.1.above
  29.2 0.0 collective-permute-done.below
  29.3 0.0 copy-done.7
  29.3 0.0 copy-done.8
  29.3 0.0 copy-done.10
  29.3 0.0 copy-done.13
  29.3 18.9 %forward_products.1 = (f32[32,80,128]{2,1,0:T(8,128)}, f32[4,48,128]{2,1,0:T(8,128)S(1)}, f32[4,2304,128]{2,1,0:T(8,128)}) custom-call(f32[4,48,128]{2,1,0:T(8,128)S(1)} %copy-done.8, f32[4,48,128]{2,1,0:T(8,128)S(1)} %copy-done.13, f32[8,128]{1,0:T(8,128)S(1)} %collective-permute-done.below, f32[8,128]{1,0:T(8,128)S(1)} %collective-permute-done.1.above, ...), custom_call_target="tpu_custom_call" | custom-call | flops 16999999488 | tf_op jit(solution)/shard_map/forward_products/pallas_call | solution.py:167
  48.2 0.0 copy-start.15
  48.2 0.6 copy-done.15
  48.8 0.0 all-to-all-done.2.packed_b
  48.8 7.4 %all-to-all-start = ((f32[32,80,128]{2,1,0:T(8,128)}), f32[32,80,128]{2,1,0:T(8,128)S(1)}, u32[]{:S(2)}, u32[]{:S(2)}) async-start(f32[32,80,128]{2,1,0:T(8,128)} %get-tuple-element.17.after), calls=%async_computation | async-start | bytes 2621440 | tf_op jit(solution)/shard_map/all_to_all | solution.py:500
  56.2 16.2 %across_products.1 = f32[32,72,128]{2,1,0:T(8,128)} custom-call(bf16[4,48,48,128]{3,2,1,0:T(8,128)(2,1)} %upper.11, f32[32,80,128]{2,1,0:T(8,128)} %get-tuple-element.17.after, f32[4,2304,128]{2,1,0:T(8,128)} %get-tuple-element.18.chain), custom_call_target="tpu_custom_call" | custom-call | flops 15000000512 | tf_op jit(solution)/shard_map/across_products/pallas_call | solution.py:220
  72.4 2.9 %all-to-all-done.packed.vectors = f32[32,80,128]{2,1,0:T(8,128)S(1)} async-done(((f32[32,80,128]{2,1,0:T(8,128)}), f32[32,80,128]{2,1,0:T(8,128)S(1)}, u32[]{:S(2)}, u32[]{:S(2)}) %all-to-all-start) | async-done | bytes 1310752 | tf_op jit(solution)/shard_map/all_to_all | solution.py:500
  75.3 0.0 copy-start.5
  75.3 6.2 %all-to-all-start.1 = ((f32[32,72,128]{2,1,0:T(8,128)}), f32[32,72,128]{2,1,0:T(8,128)}, u32[]{:S(2)}, u32[]{:S(2)}) async-start(f32[32,72,128]{2,1,0:T(8,128)} %across_products.1), calls=%async_computation.1 | async-start | bytes 2359296 | tf_op jit(solution)/shard_map/all_to_all | solution.py:500
  81.5 0.0 copy-done.5
  81.5 6.9 %forward_solve_kernel.1.states = f32[32,16,128]{2,1,0:T(8,128)} custom-call(f32[32,80,128]{2,1,0:T(8,128)} %copy-done.5, f32[32,80,128]{2,1,0:T(8,128)} %copy-done.5), custom_call_target="tpu_custom_call" | custom-call | flops 7000000000 | tf_op jit(solution)/shard_map/forward_solve_kernel/pallas_call | solution.py:488
  88.4 0.0 copy-start.3
  88.4 11.0 %all-to-all-done.1.packed.across = f32[32,72,128]{2,1,0:T(8,128)} async-done(((f32[32,72,128]{2,1,0:T(8,128)}), f32[32,72,128]{2,1,0:T(8,128)}, u32[]{:S(2)}, u32[]{:S(2)}) %all-to-all-start.1) | async-done | bytes 1179680 | tf_op jit(solution)/shard_map/all_to_all | solution.py:500
  99.4 0.0 copy-start.17
  99.4 0.9 copy-done.17
  100.3 0.0 copy-start.4
  100.3 0.0 copy-start.16
  100.3 0.0 copy-start.2
  100.3 6.6 %backward_solve_kernel.1 = f32[32,8,128]{2,1,0:T(8,128)S(1)} custom-call(f32[32,72,128]{2,1,0:T(8,128)} %all-to-all-done.1.packed.across, f32[32,72,128]{2,1,0:T(8,128)S(1)} %all-to-all-done.2.packed_b, f32[32,16,128]{2,1,0:T(8,128)S(1)} %copy-done.17), custom_call_target="tpu_custom_call" | custom-call | flops 7000000000 | tf_op jit(solution)/shard_map/backward_solve_kernel/pallas_call | solution.py:488
  106.9 12.0 %all_to_all.30 = f32[32,8,128]{2,1,0:T(8,128)S(1)} all-to-all(f32[32,8,128]{2,1,0:T(8,128)S(1)} %backward_solve_kernel.1), channel_id=1, replica_groups=mesh['surf'=4,'norm'=32] {'norm'}, dimensions={0} | all-to-all | bytes 262144 | tf_op jit(solution)/shard_map/all_to_all | solution.py:500
  118.9 0.0 copy-done.3
  118.9 0.0 copy-done.4
  118.9 0.0 copy-done.16
  118.9 0.0 copy-start
  119.0 0.0 copy-start.1
  119.0 0.0 copy-start.9
  119.0 0.0 copy-start.11
  119.0 1.2 finish.2
  120.2 0.5 collective-permute-start.2
  120.8 2.6 %collective-permute-start.3 = (f32[8,128]{1,0:T(8,128)S(1)}, f32[8,128]{1,0:T(8,128)S(1)}, u32[]{:S(2)}, u32[]{:S(2)}) collective-permute-start(f32[8,128]{1,0:T(8,128)S(1)} %get-tuple-element.22), channel_id=1, source_target_pairs={{32,0},{64,32},{96,64},{0,96},{33,1},{65,33},{97,65},{1,97},{34,2}... | collective-permute-start | bytes 12296 | tf_op jit(solution)/shard_map/ppermute | solution.py:514
  123.3 0.9 collective-permute-done.2.below
  124.3 0.0 collective-permute-done.3.above
  124.3 0.0 copy-done.2
  124.3 0.0 copy-done
  124.3 0.0 copy-done.1
  124.3 0.0 copy-done.9
  124.3 0.0 copy-done.11
  124.3 0.0 copy-start.6
  124.3 2.8 %local_source.1 = (f32[4,48,128]{2,1,0:T(8,128)S(1)}, f32[32,8,128]{2,1,0:T(8,128)S(1)}) custom-call(f32[4,48,128]{2,1,0:T(8,128)S(1)} %copy-done.9, f32[4,48,128]{2,1,0:T(8,128)S(1)} %get-tuple-element.20.delta, f32[8,128]{1,0:T(8,128)S(1)} %collective-permute-done.2.below, f32[8,128]{1,0:T(8,128)S(1)} %collective-permute-done.3.above, ...), custom_call_target="tpu_custom_call" | custom-call | flops 3000000000 | tf_op jit(solution)/shard_map/local_source/pallas_call | solution.py:317
  127.1 12.1 %all_to_all.31.vectors = f32[32,8,128]{2,1,0:T(8,128)S(1)} all-to-all(f32[32,8,128]{2,1,0:T(8,128)S(1)} %get-tuple-element.23), channel_id=1, replica_groups=mesh['surf'=4,'norm'=32] {'norm'}, dimensions={0} | all-to-all | bytes 262144 | tf_op jit(solution)/shard_map/all_to_all | solution.py:500
  139.2 0.0 copy-done.6
  139.2 9.7 %solve_both.1 = f32[32,8,128]{2,1,0:T(8,128)S(1)} custom-call(f32[32,80,128]{2,1,0:T(8,128)S(1)} %copy-done.6, f32[32,8,128]{2,1,0:T(8,128)S(1)} %all_to_all.31.vectors, f32[32,72,128]{2,1,0:T(8,128)} %all-to-all-done.1.packed.across, f32[32,72,128]{2,1,0:T(8,128)S(1)} %all-to-all-done.2.packed_b), custom_call_target="tpu_custom_call" | custom-call | flops 12000000000 | tf_op jit(solution)/shard_map/solve_both/pallas_call | solution.py:471
  148.9 11.3 %all_to_all.32 = f32[32,8,128]{2,1,0:T(8,128)S(1)} all-to-all(f32[32,8,128]{2,1,0:T(8,128)S(1)} %solve_both.1), channel_id=1, replica_groups=mesh['surf'=4,'norm'=32] {'norm'}, dimensions={0} | all-to-all | bytes 262144 | tf_op jit(solution)/shard_map/all_to_all | solution.py:500
  160.2 1.8 %finish.3 = f32[4,48,128]{2,1,0:T(8,128)} custom-call(f32[256,128]{1,0:T(8,128)S(1)} %bitcast.3, f32[4,48,128]{2,1,0:T(8,128)S(1)} %get-tuple-element.24.source, bf16[4,48,48,128]{3,2,1,0:T(8,128)(2,1)S(1)} %copy-done.3, bf16[4,48,48,128]{3,2,1,0:T(8,128)(2,1)S(1)} %copy-done.4), custom_call_target="tpu_custom_call" | custom-call | flops 1500000000 | tf_op jit(solution)/shard_map/finish/pallas_call | solution.py:350
Async XLA Ops:
  0.0 0.9 copy-start.12
  1.0 3.4 %copy-start.14 = (f32[8,128]{1,0:T(8,128)}, f32[8,128]{1,0:T(8,128)S(1)}, u32[]{:S(2)}) copy-start(f32[8,128]{1,0:T(8,128)S(1)} %get-tuple-element.16.after) | copy-start | bytes 12292
  1.0 28.2 %collective-permute-start.1 = (f32[8,128]{1,0:T(8,128)S(1)}, f32[8,128]{1,0:T(8,128)S(1)}, u32[]{:S(2)}, u32[]{:S(2)}) collective-permute-start(f32[8,128]{1,0:T(8,128)S(1)} %get-tuple-element.16.after), channel_id=1, source_target_pairs={{32,0},{64,32},{96,64},{0,96},{33,1},{65,33},{97,65},{1,97},{34,2}... | collective-permute-start | bytes 12296 | tf_op jit(solution)/shard_map/ppermute | solution.py:514
  4.4 24.9 %collective-permute-start = (f32[8,128]{1,0:T(8,128)S(1)}, f32[8,128]{1,0:T(8,128)S(1)}, u32[]{:S(2)}, u32[]{:S(2)}) collective-permute-start(f32[8,128]{1,0:T(8,128)S(1)} %get-tuple-element.15), channel_id=1, source_target_pairs={{0,32},{32,64},{64,96},{96,0},{1,33},{33,65},{65,97},{97,1},{2,34}... | collective-permute-start | bytes 12296 | tf_op jit(solution)/shard_map/ppermute | solution.py:513
  20.0 9.3 %copy-start.7 = (f32[32,72,128]{2,1,0:T(8,128)S(1)}, f32[32,72,128]{2,1,0:T(8,128)}, u32[]{:S(2)}) copy-start(f32[32,72,128]{2,1,0:T(8,128)} %backward_products.1.after) | copy-start | bytes 3538948
  20.0 9.3 %copy-start.8 = (f32[4,48,128]{2,1,0:T(8,128)S(1)}, f32[4,48,128]{2,1,0:T(8,128)}, u32[]{:S(2)}) copy-start(f32[4,48,128]{2,1,0:T(8,128)} %rhs.3) | copy-start | bytes 294916
  20.0 9.3 %copy-start.10 = (f32[4,48,128]{2,1,0:T(8,128)S(1)}, f32[4,48,128]{2,1,0:T(8,128)}, u32[]{:S(2)}) copy-start(f32[4,48,128]{2,1,0:T(8,128)} %dissipation.3) | copy-start | bytes 294916
  20.0 9.3 %copy-start.13 = (f32[4,48,128]{2,1,0:T(8,128)S(1)}, f32[4,48,128]{2,1,0:T(8,128)}, u32[]{:S(2)}) copy-start(f32[4,48,128]{2,1,0:T(8,128)} %delta.3) | copy-start | bytes 294916
  20.0 28.8 %all-to-all-start.2 = ((f32[32,72,128]{2,1,0:T(8,128)}), f32[32,72,128]{2,1,0:T(8,128)S(1)}, u32[]{:S(2)}, u32[]{:S(2)}) async-start(f32[32,72,128]{2,1,0:T(8,128)} %backward_products.1.after), calls=%async_computation.2 | async-start | bytes 2359296 | tf_op jit(solution)/shard_map/all_to_all | solution.py:500
  48.2 0.6 copy-start.15
  48.8 26.5 %all-to-all-start = ((f32[32,80,128]{2,1,0:T(8,128)}), f32[32,80,128]{2,1,0:T(8,128)S(1)}, u32[]{:S(2)}, u32[]{:S(2)}) async-start(f32[32,80,128]{2,1,0:T(8,128)} %get-tuple-element.17.after), calls=%async_computation | async-start | bytes 2621440 | tf_op jit(solution)/shard_map/all_to_all | solution.py:500
  75.3 6.2 %copy-start.5 = (f32[32,80,128]{2,1,0:T(8,128)}, f32[32,80,128]{2,1,0:T(8,128)S(1)}, u32[]{:S(2)}) copy-start(f32[32,80,128]{2,1,0:T(8,128)S(1)} %all-to-all-done.packed.vectors) | copy-start | bytes 3932164
  75.3 24.1 %all-to-all-start.1 = ((f32[32,72,128]{2,1,0:T(8,128)}), f32[32,72,128]{2,1,0:T(8,128)}, u32[]{:S(2)}, u32[]{:S(2)}) async-start(f32[32,72,128]{2,1,0:T(8,128)} %across_products.1), calls=%async_computation.1 | async-start | bytes 2359296 | tf_op jit(solution)/shard_map/all_to_all | solution.py:500
  88.4 30.5 %copy-start.3 = (bf16[4,48,48,128]{3,2,1,0:T(8,128)(2,1)S(1)}, bf16[4,48,48,128]{3,2,1,0:T(8,128)(2,1)}, u32[]{:S(2)}) copy-start(bf16[4,48,48,128]{3,2,1,0:T(8,128)(2,1)} %lower.7) | copy-start | bytes 7077892
  99.4 1.0 copy-start.17
  100.3 18.6 %copy-start.4 = (bf16[4,48,48,128]{3,2,1,0:T(8,128)(2,1)S(1)}, bf16[4,48,48,128]{3,2,1,0:T(8,128)(2,1)}, u32[]{:S(2)}) copy-start(bf16[4,48,48,128]{3,2,1,0:T(8,128)(2,1)} %upper.11) | copy-start | bytes 7077892
  100.3 18.6 %copy-start.16 = (f32[4,48,128]{2,1,0:T(8,128)S(1)}, f32[4,48,128]{2,1,0:T(8,128)}, u32[]{:S(2)}) copy-start(f32[4,48,128]{2,1,0:T(8,128)} %copy-done.15) | copy-start | bytes 294916
  100.3 23.9 %copy-start.2 = (bf16[4,48,48,128]{3,2,1,0:T(8,128)(2,1)S(1)}, bf16[4,48,48,128]{3,2,1,0:T(8,128)(2,1)}, u32[]{:S(2)}) copy-start(bf16[4,48,48,128]{3,2,1,0:T(8,128)(2,1)} %inverse.3) | copy-start | bytes 7077892
  118.9 5.3 %copy-start = (bf16[4,48,48,128]{3,2,1,0:T(8,128)(2,1)S(1)}, bf16[4,48,48,128]{3,2,1,0:T(8,128)(2,1)}, u32[]{:S(2)}) copy-start(bf16[4,48,48,128]{3,2,1,0:T(8,128)(2,1)} %minus.3) | copy-start | bytes 7077892
  119.0 5.3 %copy-start.1 = (bf16[4,48,48,128]{3,2,1,0:T(8,128)(2,1)S(1)}, bf16[4,48,48,128]{3,2,1,0:T(8,128)(2,1)}, u32[]{:S(2)}) copy-start(bf16[4,48,48,128]{3,2,1,0:T(8,128)(2,1)} %plus.3) | copy-start | bytes 7077892
  119.0 5.3 %copy-start.9 = (f32[4,48,128]{2,1,0:T(8,128)S(1)}, f32[4,48,128]{2,1,0:T(8,128)}, u32[]{:S(2)}) copy-start(f32[4,48,128]{2,1,0:T(8,128)} %rhs.3) | copy-start | bytes 294916
  119.0 5.3 %copy-start.11 = (f32[4,48,128]{2,1,0:T(8,128)S(1)}, f32[4,48,128]{2,1,0:T(8,128)}, u32[]{:S(2)}) copy-start(f32[4,48,128]{2,1,0:T(8,128)} %dissipation.3) | copy-start | bytes 294916
  120.2 4.0 %collective-permute-start.2 = (f32[8,128]{1,0:T(8,128)S(1)}, f32[8,128]{1,0:T(8,128)S(1)}, u32[]{:S(2)}, u32[]{:S(2)}) collective-permute-start(f32[8,128]{1,0:T(8,128)S(1)} %get-tuple-element.21), channel_id=1, source_target_pairs={{0,32},{32,64},{64,96},{96,0},{1,33},{33,65},{65,97},{97,1},{2,34}... | collective-permute-start | bytes 12296 | tf_op jit(solution)/shard_map/ppermute | solution.py:513
  120.8 3.5 %collective-permute-start.3 = (f32[8,128]{1,0:T(8,128)S(1)}, f32[8,128]{1,0:T(8,128)S(1)}, u32[]{:S(2)}, u32[]{:S(2)}) collective-permute-start(f32[8,128]{1,0:T(8,128)S(1)} %get-tuple-element.22), channel_id=1, source_target_pairs={{32,0},{64,32},{96,64},{0,96},{33,1},{65,33},{97,65},{1,97},{34,2}... | collective-permute-start | bytes 12296 | tf_op jit(solution)/shard_map/ppermute | solution.py:514
  124.3 14.9 %copy-start.6 = (f32[32,80,128]{2,1,0:T(8,128)S(1)}, f32[32,80,128]{2,1,0:T(8,128)}, u32[]{:S(2)}) copy-start(f32[32,80,128]{2,1,0:T(8,128)} %copy-done.5) | copy-start | bytes 3932164
